TPU v7x, 128 devices: a whole 4x4x4 slice. The times are simulated.
128 devices in a mesh: qrow: 16 (over x, z_hi, core), kvcol: 8 (over y, z_lo).
Axes of the slice: x: 4, y: 4, z: 4 (z_hi: 2, z_lo: 2; z = z_hi * 2 + z_lo), core: 2. Of those that a mesh axis runs over, the one named last changes fastest.
Arguments:
- queries: bfloat16 [8, 2048, 4096], P('kvcol', 'qrow'), may hold values from -90 to 90, as said below
- shared_kv: bfloat16 [2, 16, 1024, 512], P(None, 'qrow', 'kvcol'), may hold values from -16 to 16, as said below
- document: int32 [16384], P(('qrow', 'kvcol')), may hold values from 0 to 16777215, as said below
Outputs:
- attended: bfloat16 [8, 2048, 4096], P('kvcol', 'qrow')
Inputs may be any that keep to these rules, and one draw needn't show every extreme that they name: Document labels never fall along the tokens and differ between documents; each document holds 1 to 8192 tokens, one exactly that many. `queries`: real numbers within the stated range. `shared_kv`: real numbers within the stated range.
All inputs are finite; a program needn't handle non-finite values.
Results may differ from a plain program's by a relative error of at most 0.017.
Values may be sent and summed in bfloat16 or wider, within the bound.
A program may use at most 256 MiB of HBM per device.

v0:
```python
import jax
import jax.numpy as jnp
from jax import lax
from jax.sharding import PartitionSpec as P

HEAD = 128
Q_HEADS = 16
KV_HEADS = 4
LAYERS = 2


NEG = -1e30


def tile_terms(qrows, qpos, qdoc, keys, values, kpos, kdoc):
    rows = qrows.shape[0]
    group = Q_HEADS // KV_HEADS
    allowed = (qdoc[:, None] == kdoc[None, :]) & (kpos[None, :] <= qpos[:, None])

    def one_head_group(index):
        which = index % KV_HEADS
        qblock = lax.dynamic_slice_in_dim(qrows, index * group * HEAD, group * HEAD, 1).reshape(
            rows, group, HEAD
        )
        kblock = lax.dynamic_slice_in_dim(keys, which * HEAD, HEAD, 1)
        vblock = lax.dynamic_slice_in_dim(values, which * HEAD, HEAD, 1)
        scores = jnp.einsum(
            "rjd,kd->jrk", qblock, kblock, preferred_element_type=jnp.float32
        ) * HEAD ** (-0.5)
        scores = jnp.where(allowed[None], scores, NEG)
        top = jnp.max(scores, axis=2)
        weights = jnp.where(allowed[None], jnp.exp(scores - top[:, :, None]), 0.0)
        total = jnp.sum(weights, axis=2)
        mixed = jnp.einsum(
            "jrk,kd->rjd", weights.astype(jnp.bfloat16), vblock, preferred_element_type=jnp.float32
        ).reshape(rows, group * HEAD)
        return (mixed, total.T, top.T)

    mixed, total, top = lax.map(one_head_group, jnp.arange(LAYERS * KV_HEADS, dtype=jnp.int32))
    mixed = jnp.transpose(mixed, (1, 0, 2)).reshape(rows, -1)
    total = jnp.transpose(total, (1, 0, 2)).reshape(rows, -1)
    top = jnp.transpose(top, (1, 0, 2)).reshape(rows, -1)
    return (mixed, total, top)


def block_terms(qrows, qpos, qdoc, keys, values, kpos, kdoc):
    rows = qrows.shape[0]
    heads = LAYERS * Q_HEADS
    live = (kpos[0] <= qpos[-1]) & (kdoc[-1] >= qdoc[0])

    def compute():
        return tile_terms(qrows, qpos, qdoc, keys, values, kpos, kdoc)

    def skipped():
        return (
            jnp.zeros((rows, heads * HEAD), jnp.float32),
            jnp.zeros((rows, heads), jnp.float32),
            jnp.full((rows, heads), NEG, jnp.float32),
        )

    return lax.cond(live, compute, skipped)


def shards(queries, shared_kv, document):
    row = lax.axis_index("qrow")
    col = lax.axis_index("kvcol")
    tok = queries.shape[1]
    qchunk = tok * lax.axis_size("qrow")
    kchunk = tok * lax.axis_size("kvcol")
    docs = lax.all_gather(document, ("qrow", "kvcol"), axis=0, tiled=True)
    qall = lax.all_gather(queries, "qrow", axis=1, tiled=True)[0]
    gathered = lax.all_gather(shared_kv, "kvcol", axis=2, tiled=True)
    keys = gathered[0, 0]
    values = gathered[1, 0]
    kpos = row * kchunk + jnp.arange(kchunk, dtype=jnp.int32)
    kdoc = lax.dynamic_slice_in_dim(docs, row * kchunk, kchunk, 0)
    qbase = col * qchunk
    qdoc_all = lax.dynamic_slice_in_dim(docs, qbase, qchunk, 0)
    block = 512

    def per_block(index):
        start = index * block
        qrows = lax.dynamic_slice_in_dim(qall, start, block, 0)
        qpos = qbase + start + jnp.arange(block, dtype=jnp.int32)
        qdoc = lax.dynamic_slice_in_dim(qdoc_all, start, block, 0)
        return block_terms(qrows, qpos, qdoc, keys, values, kpos, kdoc)

    mixed, total, top = lax.map(per_block, jnp.arange(qchunk // block, dtype=jnp.int32))
    mixed = mixed.reshape(qchunk, -1)
    total = total.reshape(qchunk, -1)
    top = top.reshape(qchunk, -1)
    peak = lax.pmax(top.astype(jnp.bfloat16), "qrow").astype(top.dtype)
    factor = jnp.exp(top - peak)
    term = mixed * jnp.repeat(factor, HEAD, axis=1)
    numer = lax.psum_scatter(
        term.astype(jnp.bfloat16), "qrow", scatter_dimension=0, tiled=True
    ).astype(jnp.float32)
    denom = lax.psum_scatter(
        (total * factor).astype(jnp.bfloat16), "qrow", scatter_dimension=0, tiled=True
    ).astype(jnp.float32)
    attended = (numer / jnp.repeat(denom, HEAD, axis=1)).astype(jnp.bfloat16)
    return attended.reshape(queries.shape)


def solution(mesh):
    placed = (P("kvcol", "qrow", None), P(None, "qrow", "kvcol", None), P(("qrow", "kvcol")))
    return jax.shard_map(
        shards, mesh=mesh, in_specs=placed, out_specs=P("kvcol", "qrow", None), check_vma=False
    )
```

profile of v0, /device:TPU:39, one launch (start us, length us, event | category | flops | bytes accessed | tf_op | source)
XLA Modules:
  0.0 1225.2 jit_solution(16716056215521583217)
XLA Ops:
  6.5 0.7 all-gather.6.cloned.1.call-update
  7.3 2.3 copy.17
  9.7 258.7 %all-gather = s32[128,1,128]{2,1,0:T(1,128)S(1)} all-gather(s32[1,1,128]{2,1,0:T(1,128)} %bitcast.114), channel_id=1, replica_groups=mesh['qrow'=16,'kvcol'=8] {'qrow','kvcol'}, dimensions={0}, use_global_device_ids=true | all-gather | bytes 66048 | tf_op jit(solution)/shard_map/all_gather | solution.py:70
  268.4 1.7 slice_bitcast_fusion
  270.1 0.5 copy.18
  270.7 119.1 %while.35 = (s32[]{:T(128)}, f32[4,512,4096]{2,1,0:T(8,128)}, f32[4,512,32]{1,0,2:T(4,128)}, f32[4,512,32]{1,0,2:T(4,128)S(1)}, s32[1024]{0:T(1024)S(1)}, /*inde...) while((s32[]{:T(128)}, f32[4,512,4096]{2,1,0:T(8,128)}, ...), condition=%wide.region_7.8_spmd, body=%wide.region_0.7_spmd.sunk | while | flops 1102574080 | bytes 75320296 | solution.py:88
  270.7 0.5 slice.28
  271.2 0.5 slice.30
  271.8 0.6 dynamic_slice.68
  273.0 0.6 slice.29
  275.0 0.5 slice.31
  276.7 4.3 conditional.2
  276.8 4.3 broadcast_in_dim.74
  281.0 8.9 copy.45
  290.1 0.6 dynamic_update_slice.45
  290.8 2.1 dynamic_update_slice.44
  292.9 7.6 constant_dynamic-update-slice_fusion.4
  300.5 0.5 slice.28
  301.0 0.5 slice.30
  301.5 0.6 dynamic_slice.68
  302.8 0.6 slice.29
  304.8 0.5 slice.31
  306.5 4.3 conditional.2
  306.5 4.3 broadcast_in_dim.74
  310.8 8.9 copy.45
  319.9 0.6 dynamic_update_slice.45
  320.6 2.1 dynamic_update_slice.44
  322.7 7.6 constant_dynamic-update-slice_fusion.4
  330.3 0.5 slice.28
  330.8 0.5 slice.30
  331.3 0.6 dynamic_slice.68
  332.6 0.6 slice.29
  334.6 0.5 slice.31
  336.3 4.3 conditional.2
  336.3 4.3 broadcast_in_dim.74
  340.6 8.9 copy.45
  349.7 0.6 dynamic_update_slice.45
  350.3 2.1 dynamic_update_slice.44
  352.4 7.6 constant_dynamic-update-slice_fusion.4
  360.0 0.5 slice.28
  360.5 0.5 slice.30
  361.1 0.6 dynamic_slice.68
  362.4 0.6 slice.29
  364.3 0.5 slice.31
  366.0 4.3 conditional.2
  366.1 4.3 broadcast_in_dim.74
  370.4 8.9 copy.45
  379.4 0.6 dynamic_update_slice.45
  380.1 2.1 dynamic_update_slice.44
  382.2 7.6 constant_dynamic-update-slice_fusion.4
  389.9 0.7 convert_element_type.33
  390.6 1.0 copy.36
  391.7 602.3 %all-reduce.2.cloned.1.call-done = bf16[2048,32]{0,1:T(8,128)(2,1)} async-done(((bf16[2048,32]{0,1:T(8,128)(2,1)}), bf16[2048,32]{0,1:T(8,128)(2,1)}) %all-reduce.2.cloned.1.call-update) | async-done | bytes 131088 | tf_op jit(solution)/shard_map/pmax | solution.py:92
  994.0 1.0 multiply_convert_fusion
  995.0 1.0 copy.26
  996.0 0.2 reduce-scatter.5.cloned.1.call-start
  996.2 0.3 copy.21
  996.5 22.3 %broadcast_in_dim.90 = f32[2048,32,128]{2,1,0:T(8,128)} broadcast(f32[2048,32]{1,0:T(8,128)S(1)} %copy.21), dimensions={0,1} | broadcast | bytes 33816576 | tf_op jit(solution)/shard_map/broadcast_in_dim | solution.py:94
  1018.9 34.4 %fusion.18 = bf16[2048,4096]{1,0:T(8,128)(2,1)} fusion(f32[256,8,32,128]{3,2,1,0:T(8,128)} %bitcast.102, f32[4,512,4096]{2,1,0:T(8,128)} %get-tuple-element.246), kind=kLoop, calls=%fused_computation.27 | loop fusion | flops 16777216 | bytes 83886080 | tf_op jit(solution)/shard_map/convert_element_type | solution.py:96
  1053.3 10.1 reduce-scatter.7.cloned.1.call-done
  1063.4 0.8 copy.27
  1064.3 150.2 %reduce-scatter.5.cloned.1.call-done = bf16[128,4096]{1,0:T(8,128)(2,1)} async-done(((bf16[2048,4096]{1,0:T(8,128)(2,1)}), bf16[128,4096]{1,0:T(8,128)(2,1)}) %reduce-scatter.5.cloned.1.call-update) | async-done | bytes 1048592 | tf_op jit(solution)/shard_map/reduce_scatter | solution.py:95
  1214.5 0.6 broadcast_in_dim.91
  1215.1 3.5 fusion.20
  (43 shorter events, 1.4 us)
Async XLA Ops:
  6.5 261.9 %all-gather.6.cloned.1.call-start = ((), (), s32[]{:S(2)}) async-start(), calls=%async_computation.3 | async-start | bytes 2359296 | tf_op jit(solution)/shard_map/all_gather | solution.py:72
  7.3 263.4 %all-gather.4.cloned.1.call-start = ((), (), s32[]{:S(2)}) async-start(), calls=%async_computation.2 | async-start | bytes 17825792 | tf_op jit(solution)/shard_map/all_gather | solution.py:71
  9.6 984.4 %all-reduce.2.cloned.1.call-start = ((), (), s32[]{:S(2)}) async-start(), calls=%async_computation.4 | async-start | bytes 262144 | tf_op jit(solution)/shard_map/pmax | solution.py:92
  390.6 672.8 %reduce-scatter.7.cloned.1.call-start = ((), (), s32[]{:S(2)}) async-start(), calls=%async_computation.6 | async-start | bytes 557056
  996.0 218.6 %reduce-scatter.5.cloned.1.call-start = ((), (), s32[]{:S(2)}) async-start(), calls=%async_computation.5 | async-start | bytes 17825792 | tf_op jit(solution)/shard_map/reduce_scatter | solution.py:95
Sparse Core Ops, SparseCore 0:
  9.0 52.7 all-gather.5
  64.1 122.8 all-gather.3
  390.7 603.2 all-reduce.1
  998.1 65.2 reduce-scatter.6
  1067.6 146.8 reduce-scatter.4
where the time goes:
time: 1230 us
  waiting for transfers between devices  763 us (62%)
  blocking collectives  259 us (21%)
  local copies, waits for them, and re-layouts  137 us (11%)
  other arithmetic  39.6 us (3%)
  between operations  13.2 us (1%)
  loops' own time  12.8 us (1%)
    pmax x1, waiting for transfers between devices, shards(): peak = lax.pmax(top.astype(jnp.bfloat16), 'qrow').astype(top.dtype)  602 us
    all_gather x1, blocking collectives, shards(): docs = lax.all_gather(document, ('qrow', 'kvcol'), axis=0, tiled=True)  259 us
    reduce_scatter x1, waiting for transfers between devices, shards(): lax.psum_scatter(term.astype(jnp.bfloat16), 'qrow', scatter_dimension=0,...  150 us
    dynamic_update_slice x24, local copies, waits for them, and re-layouts, shards(): lax.map(per_block, jnp.arange(qchunk // block, dtype=jnp.int32))  77.7 us
    convert_element_type x1, other arithmetic, shards(): term.astype(jnp.bfloat16)  34.4 us
  transfers between devices with their start and end apart: 5, of which 3 were waited for; matrix products, arithmetic and copies ran while one was open for 5% of the time, Pallas kernels for 0%

commit v1 on v0

v1 whole, which is shorter than its diff:
```python
import functools
import jax
import jax.numpy as jnp
from jax import lax
from jax.experimental import pallas as pl
from jax.experimental.pallas import tpu as pltpu
from jax.sharding import PartitionSpec as P

HEAD = 128
Q_HEADS = 16
KV_HEADS = 4
LAYERS = 2
GROUP = Q_HEADS // KV_HEADS
TOK = 128
MESH = pl.DeviceIdType.MESH


def place():
    row, col = lax.axis_index("qrow"), lax.axis_index("kvcol")
    return row // 4, col // 2, ((row // 2) % 2) * 2 + col % 2, row % 2


def row_of(x, z, core):
    return (x * 2 + z // 2) * 2 + core


def device(x, y, z, core):
    return (row_of(x, z, core), y * 2 + z % 2)


def greet(devices):
    barrier = pltpu.get_barrier_semaphore()
    for d in devices:
        pl.semaphore_signal(barrier, inc=1, device_id=d, device_id_type=MESH)
    pl.semaphore_wait(barrier, len(devices))


class Copies:
    def __init__(self, send_sem, recv_sem):
        self.send_sem, self.recv_sem, self.started = send_sem, recv_sem, []

    def send(self, src, dst, to):
        n = len(self.started)
        copy = pltpu.make_async_remote_copy(
            src_ref=src, dst_ref=dst, send_sem=self.send_sem.at[n], recv_sem=self.recv_sem.at[n],
            device_id=to, device_id_type=MESH,
        )
        copy.start()
        self.started.append(copy)
        return copy

    def finish(self):
        for copy in self.started:
            copy.wait_send()


GATHER_COPIES = 3 + 6 + 2 * (4 * 2 + 4 + 4 * 2 + 4 * 2) + 32


def gather_kernel(q_ref, kv_ref, qx_ref, kvx_ref, send_sem, recv_sem, here_sem):
    x, y, z, core = place()
    col = lax.axis_index("kvcol")
    row = lax.axis_index("qrow")
    nx = [(x + 1) % 4, (x + 3) % 4]
    nz = [(z + 1) % 4, (z + 3) % 4]
    ys = [(y + k) % 4 for k in range(4)]
    beside = device(x, y, z, 1 - core)
    legs = {0: [device(v, y, z, core) for v in nx], 1: [device(x, y, v, core) for v in nz]}
    greet(legs[0] + legs[1] + [beside] + [device(x, ys[k], z, core) for k in (1, 2, 3)])

    copies = Copies(send_sem, recv_sem)

    def part(half, bx, bz, which):
        return kvx_ref.at[half, row_of(bx, bz, core), which, bz % 2]

    def head_slice(ref, index, width):
        return ref.at[:, pl.ds(pl.multiple_of(index * width, width), width)]

    every = pl.ds(0, 4)
    own = [head_slice(kv_ref.at[h], y, HEAD) for h in (0, 1)]
    local = []
    for h in (0, 1):
        c = pltpu.make_async_copy(own[h], part(h, x, z, y), here_sem.at[h])
        c.start()
        local.append(c)
    first = {}
    for h in (0, 1):
        for way in (0, 1):
            first[h, 0, way] = copies.send(own[h], part(h, x, z, y), legs[h][way])
    across = {}
    for k in (1, 3, 2):
        src = kv_ref.at[:, :, pl.ds(pl.multiple_of(ys[k] * HEAD, HEAD), HEAD)]
        across[k] = copies.send(src, kvx_ref.at[:, row, y, z % 2], device(x, ys[k], z, core))
    width = GROUP * HEAD
    asked = []
    for layer in range(LAYERS):
        c = pltpu.make_async_copy(
            head_slice(q_ref, layer * KV_HEADS + y, width), qx_ref.at[y, layer], here_sem.at[2 + layer])
        c.start()
        local.append(c)
    for k in (1, 3, 2):
        for layer in range(LAYERS):
            asked.append(copies.send(
                head_slice(q_ref, layer * KV_HEADS + ys[k], width), qx_ref.at[y, layer], device(x, ys[k], z, core)))
    for k in (1, 3, 2):
        across[k].wait_recv()
        for h in (0, 1):
            ref = part(h, x, z, (y + 4 - k) % 4)
            for way in (0, 1):
                first[h, k, way] = copies.send(ref, ref, legs[h][way])
    for c in local[:2]:
        c.wait()

    given = []

    def share(half, bx, bz):
        ref = part(half, bx, bz, every)
        given.append(copies.send(ref, ref, beside))

    second = {}

    def onward(half, step, bx, bz):
        ref = part(half, bx, bz, every)
        for way in (0, 1):
            second[half, step, way] = copies.send(ref, ref, legs[1 - half][way])
        share(half, bx, bz)

    def came(half, way):
        if half == 0:
            return (nx[1 - way], z)
        return (x, nz[1 - way])

    for h in (0, 1):
        onward(h, 0, x, z)
    further = {}
    for k in (0, 1, 3, 2):
        way = 0 if k < 2 else 1
        for h in (0, 1):
            first[h, k, way].wait_recv()
            ref = part(h, *came(h, way), (y + 4 - k) % 4)
            further[h, k] = copies.send(ref, ref, legs[h][way])
    for way in (0, 1):
        for k in ((2, 3), (0, 1))[way]:
            for h in (0, 1):
                first[h, k, way].wait_recv()
        for h in (0, 1):
            onward(h, 1 + way, *came(h, way))
    for h in (0, 1):
        for k in range(4):
            further[h, k].wait_recv()
        opposite = ((x + 2) % 4, z) if h == 0 else (x, (z + 2) % 4)
        onward(h, 3, *opposite)

    def row_block(half, step):
        if half == 0:
            return [x, nx[1], nx[0], (x + 2) % 4][step]
        return [z, nz[1], nz[0], (z + 2) % 4][step]

    last = {}
    for step in range(4):
        for h in (0, 1):
            for way in (0, 1):
                second[h, step, way].wait_recv()
                b = row_block(h, step)
                bx, bz = (b, nz[1 - way]) if h == 0 else (nx[1 - way], b)
                ref = part(h, bx, bz, pl.ds(2 * way, 2))
                last[h, step, way] = copies.send(ref, ref, legs[1 - h][way])
                share(h, bx, bz)
    for step in range(4):
        for h in (0, 1):
            for way in (0, 1):
                last[h, step, way].wait_recv()
            b = row_block(h, step)
            share(h, *((b, (z + 2) % 4) if h == 0 else ((x + 2) % 4, b)))
    for c in given:
        c.wait_recv()
    for c in asked:
        c.wait_recv()
    for c in local[2:]:
        c.wait()
    copies.finish()


def gather(q, kv):
    anywhere = pl.BlockSpec(memory_space=pl.ANY)
    return pl.pallas_call(
        gather_kernel,
        out_shape=[
            jax.ShapeDtypeStruct((KV_HEADS, LAYERS, TOK, GROUP * HEAD), q.dtype),
            jax.ShapeDtypeStruct((2, 16, 4, 2, TOK, HEAD), kv.dtype),
        ],
        in_specs=[anywhere] * 2,
        out_specs=[anywhere] * 2,
        scratch_shapes=[
            pltpu.SemaphoreType.DMA((GATHER_COPIES,)),
            pltpu.SemaphoreType.DMA((GATHER_COPIES,)),
            pltpu.SemaphoreType.DMA((4,)),
        ],
        compiler_params=pltpu.CompilerParams(collective_id=0, has_side_effects=True),
    )(q, kv)


def return_kernel(o_ref, out_ref, send_sem, recv_sem, here_sem):
    x, y, z, core = place()
    ys = [(y + k) % 4 for k in range(4)]
    others = [device(x, ys[k], z, core) for k in (1, 3, 2)]
    greet(others)
    copies = Copies(send_sem, recv_sem)
    width = GROUP * HEAD

    def mine(layer):
        return out_ref.at[:, pl.ds(pl.multiple_of((layer * KV_HEADS + y) * width, width), width)]

    for k, to in zip((1, 3, 2), others):
        for layer in range(LAYERS):
            copies.send(o_ref.at[ys[k], layer], mine(layer), to)
    local = [pltpu.make_async_copy(o_ref.at[y, layer], mine(layer), here_sem.at[layer]) for layer in range(LAYERS)]
    for c in local:
        c.start()
    for c in local:
        c.wait()
    for c in copies.started:
        c.wait_recv()
    copies.finish()


def give_back(o):
    anywhere = pl.BlockSpec(memory_space=pl.ANY)
    return pl.pallas_call(
        return_kernel,
        out_shape=jax.ShapeDtypeStruct((TOK, LAYERS * Q_HEADS * HEAD), o.dtype),
        in_specs=[anywhere],
        out_specs=anywhere,
        scratch_shapes=[
            pltpu.SemaphoreType.DMA((6,)),
            pltpu.SemaphoreType.DMA((6,)),
            pltpu.SemaphoreType.DMA((2,)),
        ],
        compiler_params=pltpu.CompilerParams(collective_id=1, has_side_effects=True),
    )(o)


SCALE = 1.4426950408889634 * HEAD ** -0.5
NEG=-1e30
BIG = 100.0
KB = 512

def attend_kernel(kb, rg, start_ref, same_ref, longest_ref, chunk_ref, q_ref, docs_ref, kv_ref, o_ref, k_buf, v_buf, q_buf, acc, top, sem):
    tiles = q_ref.shape[0]
    heads = LAYERS*GROUP
    rows = heads*TOK
    total = kv_ref.shape[1]
    piece = total//tiles
    for i in range(tiles):
        src = pl.ds(i*piece, piece); dst = pl.ds(kb + i*piece, piece)
        pltpu.make_async_copy(kv_ref.at[0, src], k_buf.at[dst], sem.at[0, i]).start()
        pltpu.make_async_copy(kv_ref.at[1, src], v_buf.at[dst], sem.at[1, i]).start()
    k_buf[0:kb] = jnp.zeros((kb, HEAD), k_buf.dtype)
    v_buf[0:kb] = jnp.zeros((kb, HEAD), v_buf.dtype)
    ones = jnp.ones((kb, HEAD), v_buf.dtype)
    sub = kb//TOK

    for t in range(tiles):
        src = pl.ds(t*piece, piece); dst = pl.ds(kb + t*piece, piece)
        for l in range(LAYERS):
            for h in range(GROUP):
                q_buf[pl.ds((l*GROUP+h)*TOK, TOK), :] = q_ref[t, l, :, h*HEAD:(h+1)*HEAD]
        length = jnp.float32(0)
        for g in range(heads):
            qf = q_buf[pl.ds(g*TOK, TOK), :].astype(jnp.float32)
            length = jnp.maximum(length, jnp.max(jnp.sum(qf*qf, axis=1, keepdims=True)))
        small = length*longest_ref[0] <= (BIG/SCALE)**2
        chunk = chunk_ref[t]
        end = (chunk + 1)*TOK
        first = start_ref[t]
        span = end - first
        blocks = (span + kb - 1)//kb
        full = jnp.where(same_ref[t] == 1, jnp.maximum(span//kb, 1), 1)
        qd = jnp.transpose(jnp.broadcast_to(docs_ref[pl.ds(chunk + sub, 1), :], (TOK, TOK)))
        pltpu.make_async_copy(kv_ref.at[0, src], k_buf.at[dst], sem.at[0, t]).wait()
        pltpu.make_async_copy(kv_ref.at[1, src], v_buf.at[dst], sem.at[1, t]).wait()
        acc[...] = jnp.zeros_like(acc)
        tri = lax.broadcasted_iota(jnp.int32, (TOK, TOK), 1) <= lax.broadcasted_iota(jnp.int32, (TOK, TOK), 0)

        def allowed(i):
            parts = []
            base = chunk + 1 - (i+1)*sub + sub
            for s in range(sub):
                kd = docs_ref[pl.ds(base + s, 1), :]
                m = qd == kd
                if s == sub-1:
                    m = m & (tri | (i > 0))
                parts.append(m)
            return jnp.concatenate(parts, axis=1)

        def quick(i, masked):
            at = pl.multiple_of(end - (i+1)*kb + kb, TOK)
            k = k_buf[pl.ds(at, kb), :]
            v = jnp.concatenate([v_buf[pl.ds(at, kb), :], ones], axis=1)
            if masked:
                mask = allowed(i)
            for g in range(rows//rg):
                r = pl.ds(g*rg, rg)
                s = lax.dot_general(q_buf[r, :], k, (((1,),(1,)),((),())), preferred_element_type=jnp.float32)
                p = jnp.exp2(s*SCALE)
                if masked:
                    p = jnp.where(jnp.concatenate([mask]*(rg//TOK), axis=0), p, 0.0)
                acc[r, :] += jnp.dot(p.astype(jnp.bfloat16), v, preferred_element_type=jnp.float32)

        def careful(i, masked):
            at = pl.multiple_of(end - (i+1)*kb + kb, TOK)
            k = k_buf[pl.ds(at, kb), :]
            v = jnp.concatenate([v_buf[pl.ds(at, kb), :], ones], axis=1)
            mask = allowed(i)
            for g in range(rows//TOK):
                r = pl.ds(g*TOK, TOK)
                s = lax.dot_general(q_buf[r, :], k, (((1,),(1,)),((),())), preferred_element_type=jnp.float32)*SCALE
                s = jnp.where(mask, s, NEG)
                old = top[r, :]
                new = jnp.maximum(old, jnp.max(s, axis=1, keepdims=True))
                top[r, :] = new
                p = jnp.where(mask, jnp.exp2(s - new[:, :1]), 0.0)
                keep = jnp.exp2(old - new)
                acc[r, :] = acc[r, :]*jnp.concatenate([keep, keep], axis=1) + jnp.dot(p.astype(jnp.bfloat16), v, preferred_element_type=jnp.float32)

        def at_masked(idx):
            return jnp.where(idx == 0, 0, idx - 1 + full)

        @pl.when(small)
        def _():
            lax.fori_loop(0, 1 + blocks - jnp.minimum(full, blocks), lambda n, _: quick(at_masked(n), True), None)
            lax.fori_loop(1, full, lambda n, _: quick(n, False), None)

        @pl.when(jnp.logical_not(small))
        def _():
            top[...] = jnp.full_like(top, NEG)
            lax.fori_loop(0, blocks, lambda n, _: careful(n, True), None)

        for l in range(LAYERS):
            for h in range(GROUP):
                r = pl.ds((l*GROUP+h)*TOK, TOK)
                a = acc[r, :]
                o_ref[t, l, :, h*HEAD:(h+1)*HEAD] = (a[:, :HEAD]/a[:, HEAD:]).astype(o_ref.dtype)

def attend(start, same, longest, chunk, q, docs, kv, kb=KB, rg=256):
    tiles = q.shape[0]
    rows = LAYERS*GROUP*TOK
    total = kv.shape[1]
    smem = pl.BlockSpec(memory_space=pltpu.SMEM)
    vmem = pl.BlockSpec(memory_space=pltpu.VMEM)
    return pl.pallas_call(
        functools.partial(attend_kernel, kb, rg),
        out_shape=jax.ShapeDtypeStruct(q.shape, q.dtype),
        in_specs=[smem]*4 + [vmem, vmem, pl.BlockSpec(memory_space=pl.ANY)],
        out_specs=vmem,
        scratch_shapes=[
            pltpu.VMEM((kb + total, HEAD), jnp.bfloat16),
            pltpu.VMEM((kb + total, HEAD), jnp.bfloat16),
            pltpu.VMEM((rows, HEAD), jnp.bfloat16),
            pltpu.VMEM((rows, 2*HEAD), jnp.float32),
            pltpu.VMEM((rows, HEAD), jnp.float32),
            pltpu.SemaphoreType.DMA((2, tiles)),
        ],
        compiler_params=pltpu.CompilerParams(vmem_limit_bytes=50*2**20),
    )(start, same, longest, chunk, q, docs, kv)


def shards(queries, shared_kv, document):
    row, col = lax.axis_index("qrow"), lax.axis_index("kvcol")
    mine = col // 2
    q = queries[0]
    kv = shared_kv[:, 0]
    keys = kv[0].astype(jnp.float32).reshape(TOK, KV_HEADS, HEAD)
    longest = jnp.ceil(jnp.max(jnp.sum(keys * keys, axis=2), axis=0)).astype(jnp.int32)
    note = jnp.concatenate([document, longest, jnp.zeros((TOK - KV_HEADS,), jnp.int32)])
    notes = lax.all_gather(note, ("qrow", "kvcol"), axis=0, tiled=False)
    docs = notes[:, :TOK]
    longest = lax.dynamic_slice_in_dim(jnp.max(notes[:, TOK:TOK + KV_HEADS], axis=0), mine, 1, 0).astype(jnp.float32)
    qx, kvx = gather(q, kv)
    kvx = kvx.reshape(2, -1, HEAD)
    chunk = jnp.arange(4, dtype=jnp.int32) * 32 + (col % 2) * 16 + row
    ends = jnp.take(docs[:, ::TOK - 1], chunk, axis=0)
    start = jnp.sum((docs[None] < ends[:, 0, None, None]).astype(jnp.int32), axis=(1, 2))
    same = (ends[:, 0] == ends[:, 1]).astype(jnp.int32)
    padded = jnp.concatenate([jnp.full((KB // TOK, TOK), -1, jnp.int32), docs])
    o = attend(start, same, longest, chunk, qx, padded, kvx)
    out = give_back(o)
    return out.reshape(queries.shape)


def solution(mesh):
    placed = (P("kvcol", "qrow", None), P(None, "qrow", "kvcol", None), P(("qrow", "kvcol")))
    return jax.shard_map(
        shards, mesh=mesh, in_specs=placed, out_specs=P("kvcol", "qrow", None), check_vma=False
    )
```

time: 1230 us -> 438 us (0.36)
  waiting for transfers between devices: 763 us -> 0 us
  Pallas kernels: 0 us -> 160 us
  local copies, waits for them, and re-layouts: 137 us -> 6.01 us
  other arithmetic: 39.6 us -> 2.3 us
  loops' own time: 12.8 us -> 0 us
  between operations: 13.2 us -> 0.76 us
    pmax x1 -> x0, waiting for transfers between devices: 602 us -> none  [shards(): peak = lax.pmax(top.astype(jnp.bfloat16), 'qrow').astype(top.dtype)]
    pallas_call x0 -> x3, Pallas kernels: none -> 160 us  [the longest x1 86.4 us: gather(): pl.pallas_call(gather_kernel, out_shape=[jax.ShapeDtypeStruct((KV_HEADS,...]
    reduce_scatter x1 -> x0, waiting for transfers between devices: 150 us -> none  [shards(): lax.psum_scatter(term.astype(jnp.bfloat16), 'qrow', scatter_dimension=0,...]
    dynamic_update_slice x24 -> x0, local copies, waits for them, and re-layouts: 77.7 us -> none  [shards(): lax.map(per_block, jnp.arange(qchunk // block, dtype=jnp.int32))]
    broadcast_in_dim x14 -> x1, local copies, waits for them, and re-layouts: 40.1 us -> 0.01 us  [shards(): jnp.zeros((TOK - KV_HEADS,), jnp.int32)]
    convert_element_type x3 -> x2, other arithmetic: 36 us -> 0.01 us  [the longest x1 0.01 us: shards(): jnp.ceil(jnp.max(jnp.sum(keys * keys, axis=2), axis=0)).astype(jnp.int32)]
    another operation x5 -> x0, loops' own time: 12.8 us -> none  [the longest x1 12.7 us: shards(): lax.map(per_block, jnp.arange(qchunk // block, dtype=jnp.int32))]
  transfers between devices with their start and end apart: 5 -> 0, of which waited for: 3 -> 0; matrix products, arithmetic and copies ran while one was open for 5% -> 0% of each run, Pallas kernels for 0% -> 0%
where the time goes in v1:
time: 438 us; the launch traced here: 429 us
  blocking collectives  260 us (59%)
  Pallas kernels  160 us (37%)
  local copies, waits for them, and re-layouts  6.01 us (1%)
    all_gather x1, blocking collectives, shards(): notes = lax.all_gather(note, ('qrow', 'kvcol'), axis=0, tiled=False)  260 us
    pallas_call x1, Pallas kernels, gather(): pl.pallas_call(gather_kernel, out_shape=[jax.ShapeDtypeStruct((KV_HEADS,...  86.4 us
    pallas_call x1, Pallas kernels, attend(): pl.pallas_call(functools.partial(attend_kernel, kb, rg), out_shape=jax.Sh...  55.7 us
    pallas_call x1, Pallas kernels, give_back(): pl.pallas_call(return_kernel, out_shape=jax.ShapeDtypeStruct((TOK, LAYERS...  18.1 us

profile of v1, /device:TPU:39, one launch (start us, length us, event | category | flops | bytes accessed | tf_op | source)
XLA Modules:
  0.0 429.5 jit_solution(7315859645916482523)
XLA Ops:
  0.0 0.9 convert_multiply_fusion
  1.0 0.1 mul.28
  1.1 0.2 reduce_sum.18
  1.3 0.7 pad_add_fusion
  2.1 260.3 %all-gather.1 = s32[128,1,256]{2,1,0:T(1,128)S(1)} all-gather(s32[1,1,256]{2,1,0:T(1,128)S(1)} %bitcast.18), channel_id=2, replica_groups=mesh['qrow'=16,'kvcol'=8] {'qrow','kvcol'}, dimensions={0}, use_global_device_ids=true | all-gather | bytes 132096 | tf_op jit(solution)/shard_map/all_gather | solution.py:376
  262.4 0.6 dynamic_slice.3
  263.7 0.1 slice.22
  263.8 0.6 gather_fusion
  264.3 0.1 broadcast_select_fusion
  264.4 0.2 slice_reduce_fusion.1
  264.6 0.2 convert_reduce_fusion.start_ref
  264.9 86.4 %shard_map.37 = (bf16[4,2,128,512]{3,2,1,0:T(8,128)(2,1)}, bf16[2,16,4,2,128,128]{5,4,3,2,1,0:T(8,128)(2,1)}) custom-call(bf16[128,4096]{1,0:T(8,128)(2,1)} %bitcast.14, bf16[2,128,512]{2,1,0:T(8,128)(2,1)} %bitcast.15), custom_call_target="tpu_custom_call" | custom-call | tf_op jit(solution)/shard_map/pallas_call | solution.py:186
  351.2 0.0 copy-start.1
  351.3 1.2 copy-done.1
  352.5 55.7 %shard_map.38.o_ref = bf16[4,2,128,512]{3,2,1,0:T(8,128)(2,1)S(1)} custom-call(s32[4]{0:T(128)S(1)} %convert_reduce_fusion.start_ref, s32[4]{0:T(128)S(1)} %compare_convert_fusion.same_ref, f32[1]{0:T(128)S(6)} %convert_element_type.25.longest_ref, s32[4]{0:T(128)S(1)} %get-tuple-element.12.chunk_ref, bf16[4,2,128,512]{3,2,1,0:T(8,128)(2,1)S(1)} %copy-done.1, ...), custom_call_target="tpu_custom_call" | custom-call | tf_op jit(solution)/shard_map/pallas_call | solution.py:351
  408.1 0.0 copy-start
  408.1 1.0 copy-done
  409.1 18.1 %shard_map.39 = bf16[128,4096]{1,0:T(8,128)(2,1)} custom-call(bf16[4,2,128,512]{3,2,1,0:T(8,128)(2,1)} %copy-done), custom_call_target="tpu_custom_call" | custom-call | tf_op jit(solution)/shard_map/pallas_call | solution.py:229
  427.2 2.3 copy.10
  (11 shorter events, 0.1 us)
Async XLA Ops:
  351.2 1.2 copy-start.1
  408.1 1.0 copy-start

commit v2 on v1

--- a/solution.py
+++ b/solution.py
@@ -54,10 +54,10 @@
             copy.wait_send()
 
 
-GATHER_COPIES = 3 + 6 + 2 * (4 * 2 + 4 + 4 * 2 + 4 * 2) + 32
-
-
-def gather_kernel(q_ref, kv_ref, qx_ref, kvx_ref, send_sem, recv_sem, here_sem):
+GATHER_COPIES = 3 + 6 + 2 * (4 * 2 + 4 + 4 * 2 + 4 * 2) + 32 + 10
+
+
+def gather_kernel(q_ref, kv_ref, doc_ref, qx_ref, kvx_ref, notes_ref, k_buf, note, send_sem, recv_sem, here_sem):
     x, y, z, core = place()
     col = lax.axis_index("kvcol")
     row = lax.axis_index("qrow")
@@ -66,7 +66,9 @@
     ys = [(y + k) % 4 for k in range(4)]
     beside = device(x, y, z, 1 - core)
     legs = {0: [device(v, y, z, core) for v in nx], 1: [device(x, y, v, core) for v in nz]}
-    greet(legs[0] + legs[1] + [beside] + [device(x, ys[k], z, core) for k in (1, 2, 3)])
+    xs = [device((x + k) % 4, y, z, core) for k in (1, 3, 2)]
+    zs = [device(x, y, (z + k) % 4, core) for k in (1, 3, 2)]
+    greet(xs + zs + [beside] + [device(x, ys[k], z, core) for k in (1, 2, 3)])
 
     copies = Copies(send_sem, recv_sem)
 
@@ -91,6 +93,22 @@
     for k in (1, 3, 2):
         src = kv_ref.at[:, :, pl.ds(pl.multiple_of(ys[k] * HEAD, HEAD), HEAD)]
         across[k] = copies.send(src, kvx_ref.at[:, row, y, z % 2], device(x, ys[k], z, core))
+    c = pltpu.make_async_copy(kv_ref.at[0], k_buf, here_sem.at[4])
+    c.start()
+    c.wait()
+    lane = lax.broadcasted_iota(jnp.int32, (1, TOK), 1)
+    lengths = jnp.zeros((1, TOK), jnp.int32)
+    for h in range(KV_HEADS):
+        k = k_buf[:, h * HEAD:(h + 1) * HEAD].astype(jnp.float32)
+        most = jnp.max(jnp.sum(k * k, axis=1, keepdims=True), axis=0, keepdims=True)
+        lengths = jnp.where(lane == h, most.astype(jnp.int32) + 1, lengths)
+    note[0:1, :] = doc_ref[...]
+    note[1:2, :] = lengths
+    zh, zl = z // 2, z % 2
+    c = pltpu.make_async_copy(note, notes_ref.at[x, zh, core, y, zl], here_sem.at[5])
+    c.start()
+    local.append(c)
+    told = [copies.send(note, notes_ref.at[x, zh, core, y, zl], device(x, ys[k], z, core)) for k in (1, 3, 2)]
     width = GROUP * HEAD
     asked = []
     for layer in range(LAYERS):
@@ -108,8 +126,16 @@
             ref = part(h, x, z, (y + 4 - k) % 4)
             for way in (0, 1):
                 first[h, k, way] = copies.send(ref, ref, legs[h][way])
-    for c in local[:2]:
+    for c in local[:3]:
         c.wait()
+
+    def tell(places, to):
+        for c in told:
+            c.wait_recv()
+        ref = notes_ref.at[places]
+        return [copies.send(ref, ref, d) for d in to]
+
+    told = tell((x, zh, core, every, zl), xs)
 
     given = []
 
@@ -132,6 +158,7 @@
 
     for h in (0, 1):
         onward(h, 0, x, z)
+    told = tell((every, zh, core, every, zl), zs)
     further = {}
     for k in (0, 1, 3, 2):
         way = 0 if k < 2 else 1
@@ -145,6 +172,7 @@
                 first[h, k, way].wait_recv()
         for h in (0, 1):
             onward(h, 1 + way, *came(h, way))
+    told = tell((every, slice(None), core), [beside])
     for h in (0, 1):
         for k in range(4):
             further[h, k].wait_recv()
@@ -172,32 +200,35 @@
                 last[h, step, way].wait_recv()
             b = row_block(h, step)
             share(h, *((b, (z + 2) % 4) if h == 0 else ((x + 2) % 4, b)))
-    for c in given:
+    for c in given + told:
         c.wait_recv()
     for c in asked:
         c.wait_recv()
-    for c in local[2:]:
+    for c in local[3:]:
         c.wait()
     copies.finish()
 
 
-def gather(q, kv):
+def gather(q, kv, document):
     anywhere = pl.BlockSpec(memory_space=pl.ANY)
     return pl.pallas_call(
         gather_kernel,
         out_shape=[
             jax.ShapeDtypeStruct((KV_HEADS, LAYERS, TOK, GROUP * HEAD), q.dtype),
             jax.ShapeDtypeStruct((2, 16, 4, 2, TOK, HEAD), kv.dtype),
+            jax.ShapeDtypeStruct((4, 2, 2, 4, 2, 2, TOK), jnp.int32),
         ],
-        in_specs=[anywhere] * 2,
-        out_specs=[anywhere] * 2,
+        in_specs=[anywhere] * 2 + [pl.BlockSpec(memory_space=pltpu.VMEM)],
+        out_specs=[anywhere] * 3,
         scratch_shapes=[
+            pltpu.VMEM((TOK, KV_HEADS * HEAD), kv.dtype),
+            pltpu.VMEM((2, TOK), jnp.int32),
             pltpu.SemaphoreType.DMA((GATHER_COPIES,)),
             pltpu.SemaphoreType.DMA((GATHER_COPIES,)),
-            pltpu.SemaphoreType.DMA((4,)),
+            pltpu.SemaphoreType.DMA((6,)),
         ],
         compiler_params=pltpu.CompilerParams(collective_id=0, has_side_effects=True),
-    )(q, kv)
+    )(q, kv, document)
 
 
 def return_kernel(o_ref, out_ref, send_sem, recv_sem, here_sem):
@@ -245,49 +276,64 @@
 BIG = 100.0
 KB = 512
 
-def attend_kernel(kb, rg, start_ref, same_ref, longest_ref, chunk_ref, q_ref, docs_ref, kv_ref, o_ref, k_buf, v_buf, q_buf, acc, top, sem):
+def attend_kernel(kb, rg, chunk_ref, notes_ref, q_ref, kv_ref, o_ref, k_buf, v_buf, q_buf, o_buf, acc, top, sem, q_sem, o_sem):
     tiles = q_ref.shape[0]
     heads = LAYERS*GROUP
     rows = heads*TOK
     total = kv_ref.shape[1]
     piece = total//tiles
+    sub = kb//TOK
+
+    def kv_copies(i):
+        src, dst = pl.ds(i*piece, piece), pl.ds(kb + i*piece, piece)
+        return [pltpu.make_async_copy(kv_ref.at[0, src], k_buf.at[dst], sem.at[0, i]),
+                pltpu.make_async_copy(kv_ref.at[1, src], v_buf.at[dst], sem.at[1, i])]
+
+    def q_copies(t):
+        return [pltpu.make_async_copy(q_ref.at[t, g//GROUP, :, pl.ds((g % GROUP)*HEAD, HEAD)],
+                                      q_buf.at[t, pl.ds(g*TOK, TOK)], q_sem.at[t, g]) for g in range(heads)]
+
+    def o_copies(t):
+        return [pltpu.make_async_copy(o_buf.at[t, l], o_ref.at[t, l], o_sem.at[t, l]) for l in range(LAYERS)]
+
     for i in range(tiles):
-        src = pl.ds(i*piece, piece); dst = pl.ds(kb + i*piece, piece)
-        pltpu.make_async_copy(kv_ref.at[0, src], k_buf.at[dst], sem.at[0, i]).start()
-        pltpu.make_async_copy(kv_ref.at[1, src], v_buf.at[dst], sem.at[1, i]).start()
+        for c in q_copies(i) + kv_copies(i):
+            c.start()
     k_buf[0:kb] = jnp.zeros((kb, HEAD), k_buf.dtype)
     v_buf[0:kb] = jnp.zeros((kb, HEAD), v_buf.dtype)
     ones = jnp.ones((kb, HEAD), v_buf.dtype)
-    sub = kb//TOK
+    labels = notes_ref[:, 0, :]
+    head = chunk_ref[tiles]
+    lane = lax.broadcasted_iota(jnp.int32, (1, TOK), 1)
+    longest = jnp.max(jnp.where(lane == head, jnp.max(notes_ref[:, 1, :], axis=0, keepdims=True), 0)).astype(jnp.float32)
+    tri = lax.broadcasted_iota(jnp.int32, (TOK, TOK), 1) <= lax.broadcasted_iota(jnp.int32, (TOK, TOK), 0)
 
     for t in range(tiles):
-        src = pl.ds(t*piece, piece); dst = pl.ds(kb + t*piece, piece)
-        for l in range(LAYERS):
-            for h in range(GROUP):
-                q_buf[pl.ds((l*GROUP+h)*TOK, TOK), :] = q_ref[t, l, :, h*HEAD:(h+1)*HEAD]
-        length = jnp.float32(0)
-        for g in range(heads):
-            qf = q_buf[pl.ds(g*TOK, TOK), :].astype(jnp.float32)
-            length = jnp.maximum(length, jnp.max(jnp.sum(qf*qf, axis=1, keepdims=True)))
-        small = length*longest_ref[0] <= (BIG/SCALE)**2
         chunk = chunk_ref[t]
         end = (chunk + 1)*TOK
-        first = start_ref[t]
+        mine = notes_ref[chunk, 0:1, :]
+        low = jnp.min(mine, axis=1, keepdims=True)
+        first = jnp.sum((labels < low).astype(jnp.int32))
+        same = jnp.min(mine) == jnp.max(mine)
         span = end - first
         blocks = (span + kb - 1)//kb
-        full = jnp.where(same_ref[t] == 1, jnp.maximum(span//kb, 1), 1)
-        qd = jnp.transpose(jnp.broadcast_to(docs_ref[pl.ds(chunk + sub, 1), :], (TOK, TOK)))
-        pltpu.make_async_copy(kv_ref.at[0, src], k_buf.at[dst], sem.at[0, t]).wait()
-        pltpu.make_async_copy(kv_ref.at[1, src], v_buf.at[dst], sem.at[1, t]).wait()
+        full = jnp.where(same, jnp.maximum(span//kb, 1), 1)
+        qd = jnp.transpose(jnp.broadcast_to(mine, (TOK, TOK)))
+        for c in q_copies(t) + kv_copies(t):
+            c.wait()
+        length = jnp.zeros((TOK, 1), jnp.float32)
+        for g in range(heads):
+            qf = q_buf[t, pl.ds(g*TOK, TOK), :].astype(jnp.float32)
+            length = jnp.maximum(length, jnp.sum(qf*qf, axis=1, keepdims=True))
+        small = jnp.max(length)*longest <= (BIG/SCALE)**2
         acc[...] = jnp.zeros_like(acc)
-        tri = lax.broadcasted_iota(jnp.int32, (TOK, TOK), 1) <= lax.broadcasted_iota(jnp.int32, (TOK, TOK), 0)
 
         def allowed(i):
             parts = []
-            base = chunk + 1 - (i+1)*sub + sub
+            base = chunk + 1 - (i+1)*sub
             for s in range(sub):
-                kd = docs_ref[pl.ds(base + s, 1), :]
-                m = qd == kd
+                at = base + s
+                m = (qd == notes_ref[jnp.maximum(at, 0), 0:1, :]) & (at >= 0)
                 if s == sub-1:
                     m = m & (tri | (i > 0))
                 parts.append(m)
@@ -301,7 +347,7 @@
                 mask = allowed(i)
             for g in range(rows//rg):
                 r = pl.ds(g*rg, rg)
-                s = lax.dot_general(q_buf[r, :], k, (((1,),(1,)),((),())), preferred_element_type=jnp.float32)
+                s = lax.dot_general(q_buf[t, r, :], k, (((1,),(1,)),((),())), preferred_element_type=jnp.float32)
                 p = jnp.exp2(s*SCALE)
                 if masked:
                     p = jnp.where(jnp.concatenate([mask]*(rg//TOK), axis=0), p, 0.0)
@@ -314,7 +360,7 @@
             mask = allowed(i)
             for g in range(rows//TOK):
                 r = pl.ds(g*TOK, TOK)
-                s = lax.dot_general(q_buf[r, :], k, (((1,),(1,)),((),())), preferred_element_type=jnp.float32)*SCALE
+                s = lax.dot_general(q_buf[t, r, :], k, (((1,),(1,)),((),())), preferred_element_type=jnp.float32)*SCALE
                 s = jnp.where(mask, s, NEG)
                 old = top[r, :]
                 new = jnp.maximum(old, jnp.max(s, axis=1, keepdims=True))
@@ -340,50 +386,45 @@
             for h in range(GROUP):
                 r = pl.ds((l*GROUP+h)*TOK, TOK)
                 a = acc[r, :]
-                o_ref[t, l, :, h*HEAD:(h+1)*HEAD] = (a[:, :HEAD]/a[:, HEAD:]).astype(o_ref.dtype)
-
-def attend(start, same, longest, chunk, q, docs, kv, kb=KB, rg=256):
+                o_buf[t, l, :, h*HEAD:(h+1)*HEAD] = (a[:, :HEAD]/a[:, HEAD:]).astype(o_ref.dtype)
+        for c in o_copies(t):
+            c.start()
+    for t in range(tiles):
+        for c in o_copies(t):
+            c.wait()
+
+
+def attend(chunk, notes, q, kv, kb=KB, rg=256):
     tiles = q.shape[0]
     rows = LAYERS*GROUP*TOK
     total = kv.shape[1]
-    smem = pl.BlockSpec(memory_space=pltpu.SMEM)
-    vmem = pl.BlockSpec(memory_space=pltpu.VMEM)
+    anywhere = pl.BlockSpec(memory_space=pl.ANY)
     return pl.pallas_call(
         functools.partial(attend_kernel, kb, rg),
         out_shape=jax.ShapeDtypeStruct(q.shape, q.dtype),
-        in_specs=[smem]*4 + [vmem, vmem, pl.BlockSpec(memory_space=pl.ANY)],
-        out_specs=vmem,
+        in_specs=[pl.BlockSpec(memory_space=pltpu.SMEM), pl.BlockSpec(memory_space=pltpu.VMEM), anywhere, anywhere],
+        out_specs=anywhere,
         scratch_shapes=[
             pltpu.VMEM((kb + total, HEAD), jnp.bfloat16),
             pltpu.VMEM((kb + total, HEAD), jnp.bfloat16),
-            pltpu.VMEM((rows, HEAD), jnp.bfloat16),
+            pltpu.VMEM((tiles, rows, HEAD), jnp.bfloat16),
+            pltpu.VMEM(q.shape, jnp.bfloat16),
             pltpu.VMEM((rows, 2*HEAD), jnp.float32),
             pltpu.VMEM((rows, HEAD), jnp.float32),
             pltpu.SemaphoreType.DMA((2, tiles)),
+            pltpu.SemaphoreType.DMA((tiles, LAYERS*GROUP)),
+            pltpu.SemaphoreType.DMA((tiles, LAYERS)),
         ],
         compiler_params=pltpu.CompilerParams(vmem_limit_bytes=50*2**20),
-    )(start, same, longest, chunk, q, docs, kv)
+    )(chunk, notes, q, kv)
 
 
 def shards(queries, shared_kv, document):
     row, col = lax.axis_index("qrow"), lax.axis_index("kvcol")
-    mine = col // 2
-    q = queries[0]
-    kv = shared_kv[:, 0]
-    keys = kv[0].astype(jnp.float32).reshape(TOK, KV_HEADS, HEAD)
-    longest = jnp.ceil(jnp.max(jnp.sum(keys * keys, axis=2), axis=0)).astype(jnp.int32)
-    note = jnp.concatenate([document, longest, jnp.zeros((TOK - KV_HEADS,), jnp.int32)])
-    notes = lax.all_gather(note, ("qrow", "kvcol"), axis=0, tiled=False)
-    docs = notes[:, :TOK]
-    longest = lax.dynamic_slice_in_dim(jnp.max(notes[:, TOK:TOK + KV_HEADS], axis=0), mine, 1, 0).astype(jnp.float32)
-    qx, kvx = gather(q, kv)
-    kvx = kvx.reshape(2, -1, HEAD)
-    chunk = jnp.arange(4, dtype=jnp.int32) * 32 + (col % 2) * 16 + row
-    ends = jnp.take(docs[:, ::TOK - 1], chunk, axis=0)
-    start = jnp.sum((docs[None] < ends[:, 0, None, None]).astype(jnp.int32), axis=(1, 2))
-    same = (ends[:, 0] == ends[:, 1]).astype(jnp.int32)
-    padded = jnp.concatenate([jnp.full((KB // TOK, TOK), -1, jnp.int32), docs])
-    o = attend(start, same, longest, chunk, qx, padded, kvx)
+    qx, kvx, notes = gather(queries[0], shared_kv[:, 0], document[None])
+    tiles = [t * 32 + (col % 2) * 16 + row for t in range(4)]
+    chunk = jnp.stack(tiles + [col // 2]).astype(jnp.int32)
+    o = attend(chunk, notes.reshape(-1, 2, TOK), qx, kvx.reshape(2, -1, HEAD))
     out = give_back(o)
     return out.reshape(queries.shape)
 

time: 438 us -> 121 us (0.28)
  the two profiles are of different devices: /device:TPU:39 before, /device:TPU:1 now
where the time goes in v2:
time: 121 us
  Pallas kernels  115 us (95%)
  local copies, waits for them, and re-layouts  5.46 us (5%)
    pallas_call x1, Pallas kernels, attend(): pl.pallas_call(functools.partial(attend_kernel, kb, rg), out_shape=jax.Sh...  58.5 us
    pallas_call x1, Pallas kernels, gather(): pl.pallas_call(gather_kernel, out_shape=[jax.ShapeDtypeStruct((KV_HEADS,...  41.1 us
    pallas_call x1, Pallas kernels, give_back(): pl.pallas_call(return_kernel, out_shape=jax.ShapeDtypeStruct((TOK, LAYERS...  15.6 us
    unnamed x7, local copies, waits for them, and re-layouts  5.37 us

profile of v2, /device:TPU:1, one launch (start us, length us, event | category | flops | bytes accessed | tf_op | source)
XLA Modules:
  0.0 120.6 jit_solution(14790433219342977191)
XLA Ops:
  0.0 0.1 stack.23.chunk_ref
  0.1 41.1 %shard_map.37 = (bf16[4,2,128,512]{3,2,1,0:T(8,128)(2,1)}, bf16[2,16,4,2,128,128]{5,4,3,2,1,0:T(8,128)(2,1)}, s32[4,2,2,4,2,2,128]{6,5,4,3,2,1,0:T(2,128)}) custom-call(bf16[128,4096]{1,0:T(8,128)(2,1)} %bitcast.14, bf16[2,128,512]{2,1,0:T(8,128)(2,1)} %bitcast.15, s32[1,128]{1,0:T(1,128)} %bitcast.16), custom_call_target="tpu_custom_call" | custom-call | tf_op jit(solution)/shard_map/pallas_call | solution.py:214
  41.2 0.0 copy-start.1
  41.2 1.2 %copy-done.1 = bf16[4,2,128,512]{3,2,1,0:T(8,128)(2,1)S(1)} copy-done((bf16[4,2,128,512]{3,2,1,0:T(8,128)(2,1)S(1)}, bf16[4,2,128,512]{3,2,1,0:T(8,128)(2,1)}, u32[]{:S(2)}) %copy-start.1) | copy-done | bytes 1048600
  42.4 0.0 copy-start.2
  42.4 0.9 copy-done.2
  43.3 58.5 %shard_map.38.o_ref = bf16[4,2,128,512]{3,2,1,0:T(8,128)(2,1)S(1)} custom-call(s32[5]{0:T(128)S(1)} %stack.23.chunk_ref, s32[128,2,128]{2,1,0:T(2,128)S(1)} %bitcast.11, bf16[4,2,128,512]{3,2,1,0:T(8,128)(2,1)S(1)} %copy-done.1, bf16[2,16384,128]{2,1,0:T(8,128)(2,1)} %bitcast.12), custom_call_target="tpu_custom_call" | custom-call | tf_op jit(solution)/shard_map/pallas_call | solution.py:402
  101.8 0.0 copy-start
  101.8 1.0 copy-done
  102.8 15.6 %shard_map.39 = bf16[128,4096]{1,0:T(8,128)(2,1)} custom-call(bf16[4,2,128,512]{3,2,1,0:T(8,128)(2,1)} %copy-done), custom_call_target="tpu_custom_call" | custom-call | tf_op jit(solution)/shard_map/pallas_call | solution.py:260
  118.4 2.3 %copy.5 = bf16[1,128,4096]{2,1,0:T(8,128)(2,1)} copy(bf16[1,128,4096]{2,1,0:T(8,128)(2,1)} %bitcast.13) | data formatting | bytes 2097152
Async XLA Ops:
  41.2 1.2 %copy-start.1 = (bf16[4,2,128,512]{3,2,1,0:T(8,128)(2,1)S(1)}, bf16[4,2,128,512]{3,2,1,0:T(8,128)(2,1)}, u32[]{:S(2)}) copy-start(bf16[4,2,128,512]{3,2,1,0:T(8,128)(2,1)} %get-tuple-element.9.q_ref) | copy-start | bytes 3145732
  42.4 0.9 copy-start.2
  101.8 1.0 copy-start

commit v3 on v2

--- a/solution.py
+++ b/solution.py
@@ -210,7 +210,7 @@
 
 
 def gather(q, kv, document):
-    anywhere = pl.BlockSpec(memory_space=pl.ANY)
+    anywhere = pl.BlockSpec(memory_space=pltpu.HBM)
     return pl.pallas_call(
         gather_kernel,
         out_shape=[
@@ -219,7 +219,7 @@
             jax.ShapeDtypeStruct((4, 2, 2, 4, 2, 2, TOK), jnp.int32),
         ],
         in_specs=[anywhere] * 2 + [pl.BlockSpec(memory_space=pltpu.VMEM)],
-        out_specs=[anywhere] * 3,
+        out_specs=[anywhere, pl.BlockSpec(memory_space=pltpu.VMEM), pl.BlockSpec(memory_space=pltpu.VMEM)],
         scratch_shapes=[
             pltpu.VMEM((TOK, KV_HEADS * HEAD), kv.dtype),
             pltpu.VMEM((2, TOK), jnp.int32),
@@ -227,7 +227,7 @@
             pltpu.SemaphoreType.DMA((GATHER_COPIES,)),
             pltpu.SemaphoreType.DMA((6,)),
         ],
-        compiler_params=pltpu.CompilerParams(collective_id=0, has_side_effects=True),
+        compiler_params=pltpu.CompilerParams(collective_id=0, has_side_effects=True, vmem_limit_bytes=16 * 2**20),
     )(q, kv, document)
 
 
@@ -256,18 +256,18 @@
 
 
 def give_back(o):
-    anywhere = pl.BlockSpec(memory_space=pl.ANY)
+    anywhere = pl.BlockSpec(memory_space=pltpu.HBM)
     return pl.pallas_call(
         return_kernel,
         out_shape=jax.ShapeDtypeStruct((TOK, LAYERS * Q_HEADS * HEAD), o.dtype),
         in_specs=[anywhere],
-        out_specs=anywhere,
+        out_specs=pl.BlockSpec(memory_space=pltpu.VMEM),
         scratch_shapes=[
             pltpu.SemaphoreType.DMA((6,)),
             pltpu.SemaphoreType.DMA((6,)),
             pltpu.SemaphoreType.DMA((2,)),
         ],
-        compiler_params=pltpu.CompilerParams(collective_id=1, has_side_effects=True),
+        compiler_params=pltpu.CompilerParams(collective_id=1, has_side_effects=True, vmem_limit_bytes=16 * 2**20),
     )(o)
 
 
@@ -275,19 +275,13 @@
 NEG=-1e30
 BIG = 100.0
 KB = 512
-
-def attend_kernel(kb, rg, chunk_ref, notes_ref, q_ref, kv_ref, o_ref, k_buf, v_buf, q_buf, o_buf, acc, top, sem, q_sem, o_sem):
+KI = 1024
+
+def attend_kernel(kb, ki, chunk_ref, notes_ref, q_ref, kv_ref, o_ref, q_buf, o_buf, acc, top, q_sem, o_sem):
     tiles = q_ref.shape[0]
     heads = LAYERS*GROUP
     rows = heads*TOK
-    total = kv_ref.shape[1]
-    piece = total//tiles
     sub = kb//TOK
-
-    def kv_copies(i):
-        src, dst = pl.ds(i*piece, piece), pl.ds(kb + i*piece, piece)
-        return [pltpu.make_async_copy(kv_ref.at[0, src], k_buf.at[dst], sem.at[0, i]),
-                pltpu.make_async_copy(kv_ref.at[1, src], v_buf.at[dst], sem.at[1, i])]
 
     def q_copies(t):
         return [pltpu.make_async_copy(q_ref.at[t, g//GROUP, :, pl.ds((g % GROUP)*HEAD, HEAD)],
@@ -297,96 +291,109 @@
         return [pltpu.make_async_copy(o_buf.at[t, l], o_ref.at[t, l], o_sem.at[t, l]) for l in range(LAYERS)]
 
     for i in range(tiles):
-        for c in q_copies(i) + kv_copies(i):
+        for c in q_copies(i):
             c.start()
-    k_buf[0:kb] = jnp.zeros((kb, HEAD), k_buf.dtype)
-    v_buf[0:kb] = jnp.zeros((kb, HEAD), v_buf.dtype)
-    ones = jnp.ones((kb, HEAD), v_buf.dtype)
     labels = notes_ref[:, 0, :]
     head = chunk_ref[tiles]
     lane = lax.broadcasted_iota(jnp.int32, (1, TOK), 1)
     longest = jnp.max(jnp.where(lane == head, jnp.max(notes_ref[:, 1, :], axis=0, keepdims=True), 0)).astype(jnp.float32)
-    tri = lax.broadcasted_iota(jnp.int32, (TOK, TOK), 1) <= lax.broadcasted_iota(jnp.int32, (TOK, TOK), 0)
-
+    tri = lax.broadcasted_iota(jnp.int32, (TOK, TOK), 0) <= lax.broadcasted_iota(jnp.int32, (TOK, TOK), 1)
+
+    bounds = []
     for t in range(tiles):
         chunk = chunk_ref[t]
-        end = (chunk + 1)*TOK
         mine = notes_ref[chunk, 0:1, :]
         low = jnp.min(mine, axis=1, keepdims=True)
-        first = jnp.sum((labels < low).astype(jnp.int32))
-        same = jnp.min(mine) == jnp.max(mine)
-        span = end - first
-        blocks = (span + kb - 1)//kb
-        full = jnp.where(same, jnp.maximum(span//kb, 1), 1)
-        qd = jnp.transpose(jnp.broadcast_to(mine, (TOK, TOK)))
-        for c in q_copies(t) + kv_copies(t):
+        bounds.append((chunk, jnp.sum((labels < low).astype(jnp.int32)), jnp.min(mine) == jnp.max(mine)))
+    length = jnp.zeros((TOK, 1), jnp.float32)
+    for t in range(tiles):
+        for c in q_copies(t):
             c.wait()
-        length = jnp.zeros((TOK, 1), jnp.float32)
         for g in range(heads):
             qf = q_buf[t, pl.ds(g*TOK, TOK), :].astype(jnp.float32)
             length = jnp.maximum(length, jnp.sum(qf*qf, axis=1, keepdims=True))
-        small = jnp.max(length)*longest <= (BIG/SCALE)**2
+    small = jnp.max(length)*longest <= (BIG/SCALE)**2
+
+    for t in range(tiles):
+        chunk, first, same = bounds[t]
+        end = (chunk + 1)*TOK
+        mine = notes_ref[chunk, 0:1, :]
+        span = jnp.maximum(end - first - kb, 0)
+        full = jnp.where(same, span//ki, 0)
+        edges = 1 + (span - full*ki + kb - 1)//kb
         acc[...] = jnp.zeros_like(acc)
 
-        def allowed(i):
+        def edge(n):
+            back = jnp.where(n == 0, 0, n*kb + full*ki)
             parts = []
-            base = chunk + 1 - (i+1)*sub
+            stop = chunk + 1 - back//TOK
+            start = jnp.maximum(stop - sub, 0)
             for s in range(sub):
-                at = base + s
-                m = (qd == notes_ref[jnp.maximum(at, 0), 0:1, :]) & (at >= 0)
-                if s == sub-1:
-                    m = m & (tri | (i > 0))
-                parts.append(m)
-            return jnp.concatenate(parts, axis=1)
-
-        def quick(i, masked):
-            at = pl.multiple_of(end - (i+1)*kb + kb, TOK)
-            k = k_buf[pl.ds(at, kb), :]
-            v = jnp.concatenate([v_buf[pl.ds(at, kb), :], ones], axis=1)
-            if masked:
-                mask = allowed(i)
-            for g in range(rows//rg):
-                r = pl.ds(g*rg, rg)
-                s = lax.dot_general(q_buf[t, r, :], k, (((1,),(1,)),((),())), preferred_element_type=jnp.float32)
-                p = jnp.exp2(s*SCALE)
-                if masked:
-                    p = jnp.where(jnp.concatenate([mask]*(rg//TOK), axis=0), p, 0.0)
-                acc[r, :] += jnp.dot(p.astype(jnp.bfloat16), v, preferred_element_type=jnp.float32)
-
-        def careful(i, masked):
-            at = pl.multiple_of(end - (i+1)*kb + kb, TOK)
-            k = k_buf[pl.ds(at, kb), :]
-            v = jnp.concatenate([v_buf[pl.ds(at, kb), :], ones], axis=1)
-            mask = allowed(i)
-            for g in range(rows//TOK):
+                at = start + s
+                label = jnp.transpose(jnp.broadcast_to(notes_ref[at, 0:1, :], (TOK, TOK)))
+                parts.append((label == mine) & (at < stop) & (tri | (at != chunk)))
+            return start*TOK, jnp.concatenate(parts, axis=0)
+
+        def block(start, size):
+            at = pl.ds(pl.multiple_of(start, TOK), size)
+            v = jnp.concatenate([jnp.transpose(kv_ref[1, at, :]), jnp.ones((16, size), kv_ref.dtype)], axis=0)
+            return kv_ref[0, at, :], v
+
+        def inner(n):
+            return end - kb - (n + 1)*ki
+
+        def dot_q(k, r):
+            return lax.dot_general(k, q_buf[t, r, :], (((1,), (1,)), ((), ())), preferred_element_type=jnp.float32)*SCALE
+
+        def quick(n, _):
+            k, v = block(inner(n), ki)
+            p = jnp.exp2(dot_q(k, pl.ds(0, rows)))
+            acc[...] += jnp.dot(v, p.astype(v.dtype), preferred_element_type=jnp.float32)
+
+        def quick_edge(n, _):
+            start, mask = edge(n)
+            k, v = block(start, kb)
+            p = jnp.exp2(dot_q(k, pl.ds(0, rows)))
+            p = jnp.where(jnp.concatenate([mask]*heads, axis=1), p, 0.0)
+            acc[...] += jnp.dot(v, p.astype(v.dtype), preferred_element_type=jnp.float32)
+
+        def careful(k, v, mask):
+            for g in range(heads):
                 r = pl.ds(g*TOK, TOK)
-                s = lax.dot_general(q_buf[t, r, :], k, (((1,),(1,)),((),())), preferred_element_type=jnp.float32)*SCALE
-                s = jnp.where(mask, s, NEG)
-                old = top[r, :]
-                new = jnp.maximum(old, jnp.max(s, axis=1, keepdims=True))
-                top[r, :] = new
-                p = jnp.where(mask, jnp.exp2(s - new[:, :1]), 0.0)
-                keep = jnp.exp2(old - new)
-                acc[r, :] = acc[r, :]*jnp.concatenate([keep, keep], axis=1) + jnp.dot(p.astype(jnp.bfloat16), v, preferred_element_type=jnp.float32)
-
-        def at_masked(idx):
-            return jnp.where(idx == 0, 0, idx - 1 + full)
+                s = dot_q(k, r)
+                if mask is not None:
+                    s = jnp.where(mask, s, NEG)
+                old = top[0:1, r]
+                new = jnp.maximum(old, jnp.max(s, axis=0, keepdims=True))
+                top[0:1, r] = new
+                p = jnp.exp2(s - new)
+                if mask is not None:
+                    p = jnp.where(mask, p, 0.0)
+                acc[:, r] = acc[:, r]*jnp.exp2(old - new) + jnp.dot(v, p.astype(v.dtype), preferred_element_type=jnp.float32)
+
+        def careful_full(n, _):
+            careful(*block(inner(n), ki), None)
+
+        def careful_edge(n, _):
+            start, mask = edge(n)
+            careful(*block(start, kb), mask)
 
         @pl.when(small)
         def _():
-            lax.fori_loop(0, 1 + blocks - jnp.minimum(full, blocks), lambda n, _: quick(at_masked(n), True), None)
-            lax.fori_loop(1, full, lambda n, _: quick(n, False), None)
+            lax.fori_loop(0, edges, quick_edge, None)
+            lax.fori_loop(0, full, quick, None)
 
         @pl.when(jnp.logical_not(small))
         def _():
             top[...] = jnp.full_like(top, NEG)
-            lax.fori_loop(0, blocks, lambda n, _: careful(n, True), None)
-
-        for l in range(LAYERS):
-            for h in range(GROUP):
-                r = pl.ds((l*GROUP+h)*TOK, TOK)
-                a = acc[r, :]
-                o_buf[t, l, :, h*HEAD:(h+1)*HEAD] = (a[:, :HEAD]/a[:, HEAD:]).astype(o_ref.dtype)
+            lax.fori_loop(0, edges, careful_edge, None)
+            lax.fori_loop(0, full, careful_full, None)
+
+        for g in range(heads):
+            r = pl.ds(g*TOK, TOK)
+            o = acc[:HEAD, r]/acc[HEAD:HEAD + 1, r]
+            h = g % GROUP
+            o_buf[t, g//GROUP, :, h*HEAD:(h + 1)*HEAD] = jnp.transpose(o).astype(o_buf.dtype)
         for c in o_copies(t):
             c.start()
     for t in range(tiles):
@@ -394,28 +401,24 @@
             c.wait()
 
 
-def attend(chunk, notes, q, kv, kb=KB, rg=256):
+def attend(chunk, notes, q, kv, kb=KB, ki=KI):
     tiles = q.shape[0]
     rows = LAYERS*GROUP*TOK
-    total = kv.shape[1]
-    anywhere = pl.BlockSpec(memory_space=pl.ANY)
+    anywhere = pl.BlockSpec(memory_space=pltpu.HBM)
     return pl.pallas_call(
-        functools.partial(attend_kernel, kb, rg),
+        functools.partial(attend_kernel, kb, ki),
         out_shape=jax.ShapeDtypeStruct(q.shape, q.dtype),
-        in_specs=[pl.BlockSpec(memory_space=pltpu.SMEM), pl.BlockSpec(memory_space=pltpu.VMEM), anywhere, anywhere],
+        in_specs=[pl.BlockSpec(memory_space=pltpu.SMEM), pl.BlockSpec(memory_space=pltpu.VMEM), anywhere, pl.BlockSpec(memory_space=pltpu.VMEM)],
         out_specs=anywhere,
         scratch_shapes=[
-            pltpu.VMEM((kb + total, HEAD), jnp.bfloat16),
-            pltpu.VMEM((kb + total, HEAD), jnp.bfloat16),
             pltpu.VMEM((tiles, rows, HEAD), jnp.bfloat16),
             pltpu.VMEM(q.shape, jnp.bfloat16),
-            pltpu.VMEM((rows, 2*HEAD), jnp.float32),
-            pltpu.VMEM((rows, HEAD), jnp.float32),
-            pltpu.SemaphoreType.DMA((2, tiles)),
+            pltpu.VMEM((HEAD + 16, rows), jnp.float32),
+            pltpu.VMEM((8, rows), jnp.float32),
             pltpu.SemaphoreType.DMA((tiles, LAYERS*GROUP)),
             pltpu.SemaphoreType.DMA((tiles, LAYERS)),
         ],
-        compiler_params=pltpu.CompilerParams(vmem_limit_bytes=50*2**20),
+        compiler_params=pltpu.CompilerParams(vmem_limit_bytes=40*2**20),
     )(chunk, notes, q, kv)
 
 

time: 121 us -> 108 us (0.89)
  the two profiles are of different devices: /device:TPU:1 before, /device:TPU:2 now
where the time goes in v3:
time: 108 us
  Pallas kernels  104 us (96%)
  local copies, waits for them, and re-layouts  3.89 us (4%)
    pallas_call x1, Pallas kernels, attend(): pl.pallas_call(functools.partial(attend_kernel, kb, ki), out_shape=jax.Sh...  56.3 us
    pallas_call x1, Pallas kernels, gather(): pl.pallas_call(gather_kernel, out_shape=[jax.ShapeDtypeStruct((KV_HEADS,...  36.6 us
    pallas_call x1, Pallas kernels, give_back(): pl.pallas_call(return_kernel, out_shape=jax.ShapeDtypeStruct((TOK, LAYERS...  10.9 us
    unnamed x7, local copies, waits for them, and re-layouts  3.8 us

profile of v3, /device:TPU:2, one launch (start us, length us, event | category | flops | bytes accessed | tf_op | source)
XLA Modules:
  0.0 107.7 jit_solution(15141714987657863430)
XLA Ops:
  0.0 0.1 stack.23.chunk_ref
  0.1 0.0 copy-start
  0.1 1.2 %copy-done = bf16[1,128,4096]{2,1,0:T(8,128)(2,1)S(1)} copy-done((bf16[1,128,4096]{2,1,0:T(8,128)(2,1)S(1)}, bf16[1,128,4096]{2,1,0:T(8,128)(2,1)}, u32[]{:S(2)}) %copy-start) | copy-done | bytes 1048600
  1.3 0.0 copy-start.1
  1.3 0.9 copy-done.1
  2.3 0.0 copy-start.2
  2.3 0.7 copy-done.2
  2.9 36.6 %shard_map.37 = (bf16[4,2,128,512]{3,2,1,0:T(8,128)(2,1)S(1)}, bf16[2,16,4,2,128,128]{5,4,3,2,1,0:T(8,128)(2,1)S(1)}, s32[4,2,2,4,2,2,128]{6,5,4,3,2,1,0:T(2,128)S(1)}) custom-call(bf16[128,4096]{1,0:T(8,128)(2,1)S(1)} %bitcast.13, bf16[2,128,512]{2,1,0:T(8,128)(2,1)S(1)} %bitcast.14, s32[1,128]{1,0:T(1,128)S(1)} %bitcast.16), custom_call_target="tpu_custom_call" | custom-call | tf_op jit(solution)/shard_map/pallas_call | solution.py:214
  39.5 56.3 %shard_map.38.o_ref = bf16[4,2,128,512]{3,2,1,0:T(8,128)(2,1)S(1)} custom-call(s32[5]{0:T(128)S(1)} %stack.23.chunk_ref, s32[128,2,128]{2,1,0:T(2,128)S(1)} %bitcast.15, bf16[4,2,128,512]{3,2,1,0:T(8,128)(2,1)S(1)} %get-tuple-element.9.q_ref, bf16[2,16384,128]{2,1,0:T(8,128)(2,1)S(1)} %bitcast.11), custom_call_target="tpu_custom_call" | custom-call | tf_op jit(solution)/shard_map/pallas_call | solution.py:408
  95.8 10.9 %shard_map.39 = bf16[128,4096]{1,0:T(8,128)(2,1)S(1)} custom-call(bf16[4,2,128,512]{3,2,1,0:T(8,128)(2,1)S(1)} %shard_map.38.o_ref), custom_call_target="tpu_custom_call" | custom-call | tf_op jit(solution)/shard_map/pallas_call | solution.py:260
  106.8 1.0 copy.5
Async XLA Ops:
  0.1 1.2 %copy-start = (bf16[1,128,4096]{2,1,0:T(8,128)(2,1)S(1)}, bf16[1,128,4096]{2,1,0:T(8,128)(2,1)}, u32[]{:S(2)}) copy-start(bf16[1,128,4096]{2,1,0:T(8,128)(2,1)} %param.3) | copy-start | bytes 3145732
  1.3 0.9 copy-start.1
  2.3 0.7 copy-start.2

commit v4 on v3

v4 whole, which is shorter than its diff:
```python
import functools
import jax
import jax.numpy as jnp
from jax import lax
from jax.experimental import pallas as pl
from jax.experimental.pallas import tpu as pltpu
from jax.sharding import PartitionSpec as P

HEAD = 128
Q_HEADS = 16
KV_HEADS = 4
LAYERS = 2
GROUP = Q_HEADS // KV_HEADS
TOK = 128
MESH = pl.DeviceIdType.MESH


def place():
    row, col = lax.axis_index("qrow"), lax.axis_index("kvcol")
    return row // 4, col // 2, ((row // 2) % 2) * 2 + col % 2, row % 2


def row_of(x, z, core):
    return (x * 2 + z // 2) * 2 + core


def device(x, y, z, core):
    return (row_of(x, z, core), y * 2 + z % 2)


def greet(devices):
    barrier = pltpu.get_barrier_semaphore()
    for d in devices:
        pl.semaphore_signal(barrier, inc=1, device_id=d, device_id_type=MESH)
    pl.semaphore_wait(barrier, len(devices))


class Copies:
    def __init__(self, send_sem, recv_sem):
        self.send_sem, self.recv_sem, self.started = send_sem, recv_sem, []

    def send(self, src, dst, to):
        n = len(self.started)
        copy = pltpu.make_async_remote_copy(
            src_ref=src, dst_ref=dst, send_sem=self.send_sem.at[n], recv_sem=self.recv_sem.at[n],
            device_id=to, device_id_type=MESH,
        )
        copy.start()
        self.started.append(copy)
        return copy

    def finish(self):
        for copy in self.started:
            copy.wait_send()


GATHER_COPIES = 3 + 6 + 2 * (4 * 2 + 4 + 7 * 2 + 4 * 2) + 32 + 10


def gather_kernel(q_ref, kv_ref, doc_ref, heads_ref, length_ref, kvx_ref, notes_ref, qx_ref, note, send_sem, recv_sem):
    x, y, z, core = place()
    col = lax.axis_index("kvcol")
    row = lax.axis_index("qrow")
    nx = [(x + 1) % 4, (x + 3) % 4]
    nz = [(z + 1) % 4, (z + 3) % 4]
    ys = [(y + k) % 4 for k in range(4)]
    beside = device(x, y, z, 1 - core)
    legs = {0: [device(v, y, z, core) for v in nx], 1: [device(x, y, v, core) for v in nz]}
    xs = [device((x + k) % 4, y, z, core) for k in (1, 3, 2)]
    zs = [device(x, y, (z + k) % 4, core) for k in (1, 3, 2)]
    greet(xs + zs + [beside] + [device(x, ys[k], z, core) for k in (1, 2, 3)])

    copies = Copies(send_sem, recv_sem)

    def part(half, bx, bz, which):
        return kvx_ref.at[half, row_of(bx, bz, core), which, bz % 2]

    def head_slice(ref, index, width):
        return ref.at[:, pl.ds(pl.multiple_of(index * width, width), width)]

    every = pl.ds(0, 4)
    own = [head_slice(kv_ref.at[h], y, HEAD) for h in (0, 1)]
    first = {}
    for h in (0, 1):
        for way in (0, 1):
            first[h, 0, way] = copies.send(own[h], part(h, x, z, y), legs[h][way])
    second = {}
    for h in (0, 1):
        for way in (0, 1):
            second[h, 0, way] = [copies.send(own[h], part(h, x, z, y), legs[1 - h][way])]
    across = {}
    for k in (1, 3, 2):
        src = kv_ref.at[:, :, pl.ds(pl.multiple_of(ys[k] * HEAD, HEAD), HEAD)]
        across[k] = copies.send(src, kvx_ref.at[:, row, y, z % 2], device(x, ys[k], z, core))
    for v in range(KV_HEADS):
        @pl.when(y == v)
        def _():
            for h in (0, 1):
                kvx_ref[h, row, v, z % 2] = kv_ref[h, :, v * HEAD:(v + 1) * HEAD]
            for layer in range(LAYERS):
                at = (layer * KV_HEADS + v) * GROUP * HEAD
                qx_ref[v, layer] = q_ref[:, at:at + GROUP * HEAD]

    lane = lax.broadcasted_iota(jnp.int32, (1, TOK), 1)
    lengths = jnp.zeros((1, TOK), jnp.int32)
    for h in range(KV_HEADS):
        k = kv_ref[0, :, h * HEAD:(h + 1) * HEAD].astype(jnp.float32)
        most = jnp.max(jnp.sum(k * k, axis=1, keepdims=True), axis=0, keepdims=True)
        lengths = jnp.where(lane == h, most.astype(jnp.int32) + 1, lengths)
    note[0:1, :] = doc_ref[...]
    note[1:2, :] = lengths
    zh, zl = z // 2, z % 2
    notes_ref[x, zh, core, y, zl] = note[...]
    told = [copies.send(note, notes_ref.at[x, zh, core, y, zl], device(x, ys[k], z, core)) for k in (1, 3, 2)]
    for k in (1, 3, 2):
        across[k].wait_recv()
        for h in (0, 1):
            ref = part(h, x, z, (y + 4 - k) % 4)
            for way in (0, 1):
                first[h, k, way] = copies.send(ref, ref, legs[h][way])
        for h in (0, 1):
            ref = part(h, x, z, (y + 4 - k) % 4)
            for way in (0, 1):
                second[h, 0, way].append(copies.send(ref, ref, legs[1 - h][way]))

    width = GROUP * HEAD
    asked = []
    for k in (1, 3, 2):
        for layer in range(LAYERS):
            asked.append(copies.send(
                head_slice(q_ref, layer * KV_HEADS + ys[k], width), qx_ref.at[y, layer], device(x, ys[k], z, core)))
    def tell(places, to):
        for c in told:
            c.wait_recv()
        ref = notes_ref.at[places]
        return [copies.send(ref, ref, d) for d in to]

    told = tell((x, zh, core, every, zl), xs)

    given = []

    def share(half, bx, bz):
        ref = part(half, bx, bz, every)
        given.append(copies.send(ref, ref, beside))

    def onward(half, step, bx, bz):
        ref = part(half, bx, bz, every)
        for way in (0, 1):
            second[half, step, way] = [copies.send(ref, ref, legs[1 - half][way])]
        share(half, bx, bz)

    def came(half, way):
        if half == 0:
            return (nx[1 - way], z)
        return (x, nz[1 - way])

    for h in (0, 1):
        share(h, x, z)
    further = {}
    for k in (0, 1, 3, 2):
        way = 0 if k < 2 else 1
        for h in (0, 1):
            first[h, k, way].wait_recv()
            ref = part(h, *came(h, way), (y + 4 - k) % 4)
            further[h, k] = copies.send(ref, ref, legs[h][way])
    for way in (0, 1):
        for k in ((2, 3), (0, 1))[way]:
            for h in (0, 1):
                first[h, k, way].wait_recv()
        for h in (0, 1):
            onward(h, 1 + way, *came(h, way))
    told = tell((every, zh, core, every, zl), zs)
    for h in (0, 1):
        for k in range(4):
            further[h, k].wait_recv()
        opposite = ((x + 2) % 4, z) if h == 0 else (x, (z + 2) % 4)
        onward(h, 3, *opposite)

    def row_block(half, step):
        if half == 0:
            return [x, nx[1], nx[0], (x + 2) % 4][step]
        return [z, nz[1], nz[0], (z + 2) % 4][step]

    last = {}
    for step in range(4):
        if step == 2:
            told = tell((every, slice(None), core), [beside])
        for h in (0, 1):
            for way in (0, 1):
                for c in second[h, step, way]:
                    c.wait_recv()
                b = row_block(h, step)
                bx, bz = (b, nz[1 - way]) if h == 0 else (nx[1 - way], b)
                ref = part(h, bx, bz, pl.ds(2 * way, 2))
                last[h, step, way] = copies.send(ref, ref, legs[1 - h][way])
                share(h, bx, bz)
    for c in asked:
        c.wait_recv()
    length = jnp.zeros((TOK, 1), jnp.float32)
    for t in range(4):
        for g in range(LAYERS * GROUP):
            head = qx_ref[t, g // GROUP, :, (g % GROUP) * HEAD:(g % GROUP + 1) * HEAD]
            heads_ref[t, g * TOK:(g + 1) * TOK, :] = head
            head = head.astype(jnp.float32)
            length = jnp.maximum(length, jnp.sum(head * head, axis=1, keepdims=True))
    length_ref[...] = jnp.broadcast_to(jnp.max(length, axis=0, keepdims=True), (1, TOK))
    for step in range(4):
        for h in (0, 1):
            for way in (0, 1):
                last[h, step, way].wait_recv()
            b = row_block(h, step)
            share(h, *((b, (z + 2) % 4) if h == 0 else ((x + 2) % 4, b)))
    for c in given + told:
        c.wait_recv()
    copies.finish()


def gather(q, kv, document):
    return pl.pallas_call(
        gather_kernel,
        out_shape=[
            jax.ShapeDtypeStruct((KV_HEADS, LAYERS * GROUP * TOK, HEAD), q.dtype),
            jax.ShapeDtypeStruct((1, TOK), jnp.float32),
            jax.ShapeDtypeStruct((2, 16, 4, 2, TOK, HEAD), kv.dtype),
            jax.ShapeDtypeStruct((4, 2, 2, 4, 2, 2, TOK), jnp.int32),
        ],
        in_specs=[pl.BlockSpec(memory_space=pltpu.VMEM)] * 3,
        out_specs=[pl.BlockSpec(memory_space=pltpu.VMEM)] * 4,
        scratch_shapes=[
            pltpu.VMEM((KV_HEADS, LAYERS, TOK, GROUP * HEAD), q.dtype),
            pltpu.VMEM((2, TOK), jnp.int32),
            pltpu.SemaphoreType.DMA((GATHER_COPIES,)),
            pltpu.SemaphoreType.DMA((GATHER_COPIES,)),
        ],
        compiler_params=pltpu.CompilerParams(collective_id=0, has_side_effects=True, vmem_limit_bytes=16 * 2**20),
    )(q, kv, document)


def return_kernel(o_ref, out_ref, send_sem, recv_sem):
    x, y, z, core = place()
    ys = [(y + k) % 4 for k in range(4)]
    others = [device(x, ys[k], z, core) for k in (1, 3, 2)]
    greet(others)
    copies = Copies(send_sem, recv_sem)
    width = GROUP * HEAD

    def mine(layer):
        return out_ref.at[:, pl.ds(pl.multiple_of((layer * KV_HEADS + y) * width, width), width)]

    for k, to in zip((1, 3, 2), others):
        for layer in range(LAYERS):
            copies.send(o_ref.at[ys[k], layer], mine(layer), to)
    for v in range(KV_HEADS):
        @pl.when(y == v)
        def _():
            for layer in range(LAYERS):
                at = (layer * KV_HEADS + v) * width
                out_ref[:, at:at + width] = o_ref[v, layer]
    for c in copies.started:
        c.wait_recv()
    copies.finish()


def give_back(o):
    return pl.pallas_call(
        return_kernel,
        out_shape=jax.ShapeDtypeStruct((TOK, LAYERS * Q_HEADS * HEAD), o.dtype),
        in_specs=[pl.BlockSpec(memory_space=pltpu.VMEM)],
        out_specs=pl.BlockSpec(memory_space=pltpu.VMEM),
        scratch_shapes=[
            pltpu.SemaphoreType.DMA((6,)),
            pltpu.SemaphoreType.DMA((6,)),
        ],
        compiler_params=pltpu.CompilerParams(collective_id=1, has_side_effects=True, vmem_limit_bytes=16 * 2**20),
    )(o)


SCALE = 1.4426950408889634 * HEAD ** -0.5
NEG=-1e30
BIG = 100.0
KB = 512
KI = 1024

def attend_kernel(kb, ki, chunk_ref, notes_ref, length_ref, q_ref, kv_ref, o_ref, acc, top):
    tiles = q_ref.shape[0]
    heads = LAYERS*GROUP
    rows = heads*TOK

    labels = notes_ref[:, 0, :]
    head = chunk_ref[tiles]
    lane = lax.broadcasted_iota(jnp.int32, (1, TOK), 1)
    longest = jnp.max(jnp.where(lane == head, jnp.max(notes_ref[:, 1, :], axis=0, keepdims=True), 0)).astype(jnp.float32)
    bounds = []
    for t in range(tiles):
        chunk = chunk_ref[t]
        mine = notes_ref[chunk, 0:1, :]
        low = jnp.min(mine, axis=1, keepdims=True)
        bounds.append((chunk, jnp.sum((labels < low).astype(jnp.int32))))
    small = jnp.max(length_ref[...])*longest <= (BIG/SCALE)**2

    for t in range(tiles):
        chunk, first = bounds[t]
        end = (chunk + 1)*TOK
        mine = notes_ref[chunk, 0:1, :]
        span = jnp.maximum(end - first - kb, 0)
        full = span//ki
        edges = 1 + (span - full*ki + kb - 1)//kb
        acc[...] = jnp.zeros_like(acc)
        below = jnp.transpose(jnp.broadcast_to(mine, (TOK, TOK))) < mine
        inside = end - TOK + jnp.sum(below.astype(jnp.int32), axis=0, keepdims=True)
        ahead = mine == jnp.min(mine, axis=1, keepdims=True)
        lowest = jnp.where(ahead, first, inside)
        ahead = jnp.concatenate([ahead]*heads, axis=1)
        place = end - TOK + lax.broadcasted_iota(jnp.int32, (1, TOK), 1)

        def edge(n):
            stop = end - jnp.where(n == 0, 0, n*kb + full*ki)
            start = jnp.maximum(stop - kb, 0)
            key = start + lax.broadcasted_iota(jnp.int32, (kb, TOK), 0)
            return start, (key >= lowest) & (key <= jnp.minimum(place, stop - 1))

        def block(start, size):
            at = pl.ds(pl.multiple_of(start, TOK), size)
            v = jnp.concatenate([jnp.transpose(kv_ref[1, at, :]), jnp.ones((16, size), kv_ref.dtype)], axis=0)
            return kv_ref[0, at, :], v

        def inner(n):
            return end - kb - (n + 1)*ki

        def dot_q(k, r):
            return lax.dot_general(k, q_ref[t, r, :], (((1,), (1,)), ((), ())), preferred_element_type=jnp.float32)*SCALE

        def quick(n, _):
            k, v = block(inner(n), ki)
            p = jnp.exp2(dot_q(k, pl.ds(0, rows)))
            acc[...] += jnp.dot(v, p.astype(v.dtype), preferred_element_type=jnp.float32)

        def quick_edge(n, _):
            start, mask = edge(n)
            k, v = block(start, kb)
            p = jnp.exp2(dot_q(k, pl.ds(0, rows)))
            p = jnp.where(jnp.concatenate([mask]*heads, axis=1), p, 0.0)
            acc[...] += jnp.dot(v, p.astype(v.dtype), preferred_element_type=jnp.float32)

        def careful(k, v, mask):
            for g in range(heads):
                r = pl.ds(g*TOK, TOK)
                s = dot_q(k, r)
                if mask is not None:
                    s = jnp.where(mask, s, NEG)
                old = top[0:1, r]
                new = jnp.maximum(old, jnp.max(s, axis=0, keepdims=True))
                top[0:1, r] = new
                p = jnp.exp2(s - new)
                if mask is not None:
                    p = jnp.where(mask, p, 0.0)
                acc[:, r] = acc[:, r]*jnp.exp2(old - new) + jnp.dot(v, p.astype(v.dtype), preferred_element_type=jnp.float32)

        def careful_full(n, _):
            careful(*block(inner(n), ki), None)

        def careful_edge(n, _):
            start, mask = edge(n)
            careful(*block(start, kb), mask)

        @pl.when(small)
        def _():
            lax.fori_loop(0, full, quick, None)
            acc[...] = jnp.where(ahead, acc[...], 0.0)
            lax.fori_loop(0, edges, quick_edge, None)

        @pl.when(jnp.logical_not(small))
        def _():
            top[...] = jnp.full_like(top, NEG)
            lax.fori_loop(0, full, careful_full, None)
            acc[...] = jnp.where(ahead, acc[...], 0.0)
            top[...] = jnp.where(ahead, top[...], NEG)
            lax.fori_loop(0, edges, careful_edge, None)

        for g in range(heads):
            r = pl.ds(g*TOK, TOK)
            o = acc[:HEAD, r]/acc[HEAD:HEAD + 1, r]
            h = g % GROUP
            o_ref[t, g//GROUP, :, h*HEAD:(h + 1)*HEAD] = jnp.transpose(o).astype(o_ref.dtype)


def attend(chunk, notes, length, q, kv, kb=KB, ki=KI):
    tiles, rows, _ = q.shape
    shape = (tiles, LAYERS, TOK, GROUP*HEAD)
    vmem = pl.BlockSpec(memory_space=pltpu.VMEM)
    return pl.pallas_call(
        functools.partial(attend_kernel, kb, ki),
        out_shape=jax.ShapeDtypeStruct(shape, q.dtype),
        in_specs=[pl.BlockSpec(memory_space=pltpu.SMEM)] + [vmem]*4,
        out_specs=vmem,
        scratch_shapes=[
            pltpu.VMEM((HEAD + 16, rows), jnp.float32),
            pltpu.VMEM((8, rows), jnp.float32),
        ],
        compiler_params=pltpu.CompilerParams(vmem_limit_bytes=40*2**20),
    )(chunk, notes, length, q, kv)


def shards(queries, shared_kv, document):
    row, col = lax.axis_index("qrow"), lax.axis_index("kvcol")
    heads, length, kvx, notes = gather(queries[0], shared_kv[:, 0], document[None])
    tiles = [t * 32 + (col % 2) * 16 + row for t in range(4)]
    chunk = jnp.stack(tiles + [col // 2]).astype(jnp.int32)
    o = attend(chunk, notes.reshape(-1, 2, TOK), length, heads, kvx.reshape(2, -1, HEAD))
    out = give_back(o)
    return out.reshape(queries.shape)


def solution(mesh):
    placed = (P("kvcol", "qrow", None), P(None, "qrow", "kvcol", None), P(("qrow", "kvcol")))
    return jax.shard_map(
        shards, mesh=mesh, in_specs=placed, out_specs=P("kvcol", "qrow", None), check_vma=False
    )
```

time: 108 us -> 102 us (0.944)
  the two profiles are of different devices: /device:TPU:2 before, /device:TPU:39 now
where the time goes in v4:
time: 102 us; the launch traced here: 101 us
  Pallas kernels  97.4 us (95%)
  local copies, waits for them, and re-layouts  3.89 us (4%)
    pallas_call x1, Pallas kernels, attend(): pl.pallas_call(functools.partial(attend_kernel, kb, ki), out_shape=jax.Sh...  49 us
    pallas_call x1, Pallas kernels, gather(): pl.pallas_call(gather_kernel, out_shape=[jax.ShapeDtypeStruct((KV_HEADS,...  34.5 us
    pallas_call x1, Pallas kernels, give_back(): pl.pallas_call(return_kernel, out_shape=jax.ShapeDtypeStruct((TOK, LAYERS...  14 us
    unnamed x7, local copies, waits for them, and re-layouts  3.8 us

profile of v4, /device:TPU:39, one launch (start us, length us, event | category | flops | bytes accessed | tf_op | source)
XLA Modules:
  0.0 101.3 jit_solution(14061130301515592999)
XLA Ops:
  0.0 0.1 stack.23.chunk_ref
  0.1 0.0 copy-start
  0.1 1.2 %copy-done = bf16[1,128,4096]{2,1,0:T(8,128)(2,1)S(1)} copy-done((bf16[1,128,4096]{2,1,0:T(8,128)(2,1)S(1)}, bf16[1,128,4096]{2,1,0:T(8,128)(2,1)}, u32[]{:S(2)}) %copy-start) | copy-done | bytes 1048600
  1.3 0.0 copy-start.1
  1.3 0.9 copy-done.1
  2.3 0.0 copy-start.2
  2.3 0.7 copy-done.2
  2.9 34.5 %shard_map.37 = (bf16[4,1024,128]{2,1,0:T(8,128)(2,1)S(1)}, f32[1,128]{1,0:T(1,128)S(1)}, bf16[2,16,4,2,128,128]{5,4,3,2,1,0:T(8,128)(2,1)S(1)}, s32[4,2,2,4,2,2,128]{6,5,4,3,2,1,0:T(2,128)S(1)}) custom-call(bf16[128,4096]{1,0:T(8,128)(2,1)S(1)} %bitcast.13, bf16[2,128,512]{2,1,0:T(8,128)(2,1)S(1)} %bitcast.14, s32[1,128]{1,0:T(1,128)S(1)} %bitcast.16), custom_call_target="tpu_custom_call" | custom-call | tf_op jit(solution)/shard_map/pallas_call | solution.py:219
  37.4 49.0 %shard_map.38.o_ref = bf16[4,2,128,512]{3,2,1,0:T(8,128)(2,1)S(1)} custom-call(s32[5]{0:T(128)S(1)} %stack.23.chunk_ref, s32[128,2,128]{2,1,0:T(2,128)S(1)} %bitcast.15, f32[1,128]{1,0:T(1,128)S(1)} %get-tuple-element.10.length_ref, bf16[4,1024,128]{2,1,0:T(8,128)(2,1)S(1)} %get-tuple-element.11.q_ref, bf16[2,16384,128]{2,1,0:T(8,128)(2,1)S(1)} %bitcast.11), custom_call_target="tpu_custom_call" | custom-call | tf_op jit(solution)/shard_map/pallas_call | solution.py:391
  86.3 14.0 %shard_map.39 = bf16[128,4096]{1,0:T(8,128)(2,1)S(1)} custom-call(bf16[4,2,128,512]{3,2,1,0:T(8,128)(2,1)S(1)} %shard_map.38.o_ref), custom_call_target="tpu_custom_call" | custom-call | tf_op jit(solution)/shard_map/pallas_call | solution.py:265
  100.3 1.0 copy.5
Async XLA Ops:
  0.1 1.2 %copy-start = (bf16[1,128,4096]{2,1,0:T(8,128)(2,1)S(1)}, bf16[1,128,4096]{2,1,0:T(8,128)(2,1)}, u32[]{:S(2)}) copy-start(bf16[1,128,4096]{2,1,0:T(8,128)(2,1)} %param.3) | copy-start | bytes 3145732
  1.3 0.9 copy-start.1
  2.3 0.7 copy-start.2

commit v5 on v4

--- a/solution.py
+++ b/solution.py
@@ -236,27 +236,31 @@
     )(q, kv, document)
 
 
-def return_kernel(o_ref, out_ref, send_sem, recv_sem):
+def return_kernel(o_ref, out_ref, relay, send_sem, recv_sem):
     x, y, z, core = place()
     ys = [(y + k) % 4 for k in range(4)]
-    others = [device(x, ys[k], z, core) for k in (1, 3, 2)]
-    greet(others)
+    to = [device(x, ys[k], z, core) for k in range(4)]
+    greet(to[1:])
     copies = Copies(send_sem, recv_sem)
     width = GROUP * HEAD
 
-    def mine(layer):
-        return out_ref.at[:, pl.ds(pl.multiple_of((layer * KV_HEADS + y) * width, width), width)]
-
-    for k, to in zip((1, 3, 2), others):
-        for layer in range(LAYERS):
-            copies.send(o_ref.at[ys[k], layer], mine(layer), to)
+    def span(owner, layer):
+        return out_ref.at[:, pl.ds(pl.multiple_of((layer * KV_HEADS + owner) * width, width), width)]
+
+    hops = (to[1], to[3])
+    handed = [copies.send(o_ref.at[ys[2], layer], relay.at[layer], hops[layer]) for layer in range(LAYERS)]
+    direct = [copies.send(o_ref.at[ys[k], layer], span(y, layer), to[k]) for layer in range(LAYERS) for k in (1, 3)]
     for v in range(KV_HEADS):
         @pl.when(y == v)
         def _():
             for layer in range(LAYERS):
                 at = (layer * KV_HEADS + v) * width
                 out_ref[:, at:at + width] = o_ref[v, layer]
-    for c in copies.started:
+    onward = []
+    for layer in range(LAYERS):
+        handed[layer].wait_recv()
+        onward.append(copies.send(relay.at[layer], span(ys[3 if layer == 0 else 1], layer), hops[layer]))
+    for c in direct + onward:
         c.wait_recv()
     copies.finish()
 
@@ -268,8 +272,9 @@
         in_specs=[pl.BlockSpec(memory_space=pltpu.VMEM)],
         out_specs=pl.BlockSpec(memory_space=pltpu.VMEM),
         scratch_shapes=[
-            pltpu.SemaphoreType.DMA((6,)),
-            pltpu.SemaphoreType.DMA((6,)),
+            pltpu.VMEM((LAYERS, TOK, GROUP * HEAD), o.dtype),
+            pltpu.SemaphoreType.DMA((8,)),
+            pltpu.SemaphoreType.DMA((8,)),
         ],
         compiler_params=pltpu.CompilerParams(collective_id=1, has_side_effects=True, vmem_limit_bytes=16 * 2**20),
     )(o)
@@ -298,14 +303,13 @@
         bounds.append((chunk, jnp.sum((labels < low).astype(jnp.int32))))
     small = jnp.max(length_ref[...])*longest <= (BIG/SCALE)**2
 
-    for t in range(tiles):
+    def tile(t):
         chunk, first = bounds[t]
         end = (chunk + 1)*TOK
         mine = notes_ref[chunk, 0:1, :]
         span = jnp.maximum(end - first - kb, 0)
         full = span//ki
         edges = 1 + (span - full*ki + kb - 1)//kb
-        acc[...] = jnp.zeros_like(acc)
         below = jnp.transpose(jnp.broadcast_to(mine, (TOK, TOK))) < mine
         inside = end - TOK + jnp.sum(below.astype(jnp.int32), axis=0, keepdims=True)
         ahead = mine == jnp.min(mine, axis=1, keepdims=True)
@@ -333,14 +337,17 @@
         def quick(n, _):
             k, v = block(inner(n), ki)
             p = jnp.exp2(dot_q(k, pl.ds(0, rows)))
-            acc[...] += jnp.dot(v, p.astype(v.dtype), preferred_element_type=jnp.float32)
-
-        def quick_edge(n, _):
+            acc[t] += jnp.where(ahead, jnp.dot(v, p.astype(v.dtype), preferred_element_type=jnp.float32), 0.0)
+
+        def quick_edge(n):
             start, mask = edge(n)
             k, v = block(start, kb)
             p = jnp.exp2(dot_q(k, pl.ds(0, rows)))
             p = jnp.where(jnp.concatenate([mask]*heads, axis=1), p, 0.0)
-            acc[...] += jnp.dot(v, p.astype(v.dtype), preferred_element_type=jnp.float32)
+            return jnp.dot(v, p.astype(v.dtype), preferred_element_type=jnp.float32)
+
+        def quick_more(n, _):
+            acc[t] += quick_edge(n)
 
         def careful(k, v, mask):
             for g in range(heads):
@@ -354,7 +361,7 @@
                 p = jnp.exp2(s - new)
                 if mask is not None:
                     p = jnp.where(mask, p, 0.0)
-                acc[:, r] = acc[:, r]*jnp.exp2(old - new) + jnp.dot(v, p.astype(v.dtype), preferred_element_type=jnp.float32)
+                acc[t, :, r] = acc[t, :, r]*jnp.exp2(old - new) + jnp.dot(v, p.astype(v.dtype), preferred_element_type=jnp.float32)
 
         def careful_full(n, _):
             careful(*block(inner(n), ki), None)
@@ -363,23 +370,41 @@
             start, mask = edge(n)
             careful(*block(start, kb), mask)
 
-        @pl.when(small)
-        def _():
+        def begin():
+            acc[t] = quick_edge(0)
+
+        def proceed():
             lax.fori_loop(0, full, quick, None)
-            acc[...] = jnp.where(ahead, acc[...], 0.0)
-            lax.fori_loop(0, edges, quick_edge, None)
-
-        @pl.when(jnp.logical_not(small))
-        def _():
+            lax.fori_loop(1, edges, quick_more, None)
+
+        def with_care():
+            acc[t] = jnp.zeros(acc.shape[1:], acc.dtype)
             top[...] = jnp.full_like(top, NEG)
             lax.fori_loop(0, full, careful_full, None)
-            acc[...] = jnp.where(ahead, acc[...], 0.0)
+            acc[t] = jnp.where(ahead, acc[t], 0.0)
             top[...] = jnp.where(ahead, top[...], NEG)
             lax.fori_loop(0, edges, careful_edge, None)
 
+        return begin, proceed, with_care
+
+    steps = [tile(t) for t in range(tiles)]
+
+    @pl.when(small)
+    def _():
+        for begin, _, _ in steps:
+            begin()
+        for _, proceed, _ in steps:
+            proceed()
+
+    @pl.when(jnp.logical_not(small))
+    def _():
+        for _, _, with_care in steps:
+            with_care()
+
+    for t in range(tiles):
         for g in range(heads):
             r = pl.ds(g*TOK, TOK)
-            o = acc[:HEAD, r]/acc[HEAD:HEAD + 1, r]
+            o = acc[t, :HEAD, r]/acc[t, HEAD:HEAD + 1, r]
             h = g % GROUP
             o_ref[t, g//GROUP, :, h*HEAD:(h + 1)*HEAD] = jnp.transpose(o).astype(o_ref.dtype)
 
@@ -394,7 +419,7 @@
         in_specs=[pl.BlockSpec(memory_space=pltpu.SMEM)] + [vmem]*4,
         out_specs=vmem,
         scratch_shapes=[
-            pltpu.VMEM((HEAD + 16, rows), jnp.float32),
+            pltpu.VMEM((tiles, HEAD + 16, rows), jnp.float32),
             pltpu.VMEM((8, rows), jnp.float32),
         ],
         compiler_params=pltpu.CompilerParams(vmem_limit_bytes=40*2**20),

time: 102 us -> 95.1 us (0.932)
  Pallas kernels: 97.4 us -> 90.8 us
    pallas_call x1, Pallas kernels: 14 us -> 10.1 us  [give_back(): pl.pallas_call(return_kernel, out_shape=jax.ShapeDtypeStruct((TOK, LAYERS...]
    pallas_call x1, Pallas kernels: 49 us -> 46.2 us  [attend(): pl.pallas_call(functools.partial(attend_kernel, kb, ki), out_shape=jax.Sh...]
where the time goes in v5:
time: 95.1 us; the launch traced here: 94.7 us
  Pallas kernels  90.8 us (95%)
  local copies, waits for them, and re-layouts  3.89 us (4%)
    pallas_call x1, Pallas kernels, attend(): pl.pallas_call(functools.partial(attend_kernel, kb, ki), out_shape=jax.Sh...  46.2 us
    pallas_call x1, Pallas kernels, gather(): pl.pallas_call(gather_kernel, out_shape=[jax.ShapeDtypeStruct((KV_HEADS,...  34.5 us
    pallas_call x1, Pallas kernels, give_back(): pl.pallas_call(return_kernel, out_shape=jax.ShapeDtypeStruct((TOK, LAYERS...  10.1 us
    unnamed x7, local copies, waits for them, and re-layouts  3.8 us

profile of v5, /device:TPU:39, one launch (start us, length us, event | category | flops | bytes accessed | tf_op | source)
XLA Modules:
  0.0 94.7 jit_solution(14964921752714375251)
XLA Ops:
  0.0 0.1 stack.23.chunk_ref
  0.1 0.0 copy-start
  0.1 1.2 %copy-done = bf16[1,128,4096]{2,1,0:T(8,128)(2,1)S(1)} copy-done((bf16[1,128,4096]{2,1,0:T(8,128)(2,1)S(1)}, bf16[1,128,4096]{2,1,0:T(8,128)(2,1)}, u32[]{:S(2)}) %copy-start) | copy-done | bytes 1048600
  1.3 0.0 copy-start.1
  1.3 0.9 %copy-done.1 = bf16[2,1,128,512]{3,2,1,0:T(8,128)(2,1)S(1)} copy-done((bf16[2,1,128,512]{3,2,1,0:T(8,128)(2,1)S(1)}, bf16[2,1,128,512]{3,2,1,0:T(8,128)(2,1)}, u32[]{:S(2)}) %copy-start.1) | copy-done | bytes 262168
  2.3 0.0 copy-start.2
  2.3 0.7 copy-done.2
  2.9 34.5 %shard_map.37 = (bf16[4,1024,128]{2,1,0:T(8,128)(2,1)S(1)}, f32[1,128]{1,0:T(1,128)S(1)}, bf16[2,16,4,2,128,128]{5,4,3,2,1,0:T(8,128)(2,1)S(1)}, s32[4,2,2,4,2,2,128]{6,5,4,3,2,1,0:T(2,128)S(1)}) custom-call(bf16[128,4096]{1,0:T(8,128)(2,1)S(1)} %bitcast.13, bf16[2,128,512]{2,1,0:T(8,128)(2,1)S(1)} %bitcast.14, s32[1,128]{1,0:T(1,128)S(1)} %bitcast.16), custom_call_target="tpu_custom_call" | custom-call | tf_op jit(solution)/shard_map/pallas_call | solution.py:219
  37.4 46.2 %shard_map.38.o_ref = bf16[4,2,128,512]{3,2,1,0:T(8,128)(2,1)S(1)} custom-call(s32[5]{0:T(128)S(1)} %stack.23.chunk_ref, s32[128,2,128]{2,1,0:T(2,128)S(1)} %bitcast.15, f32[1,128]{1,0:T(1,128)S(1)} %get-tuple-element.10.length_ref, bf16[4,1024,128]{2,1,0:T(8,128)(2,1)S(1)} %get-tuple-element.11.q_ref, bf16[2,16384,128]{2,1,0:T(8,128)(2,1)S(1)} %bitcast.11), custom_call_target="tpu_custom_call" | custom-call | tf_op jit(solution)/shard_map/pallas_call | solution.py:416
  83.6 10.1 %shard_map.39 = bf16[128,4096]{1,0:T(8,128)(2,1)S(1)} custom-call(bf16[4,2,128,512]{3,2,1,0:T(8,128)(2,1)S(1)} %shard_map.38.o_ref), custom_call_target="tpu_custom_call" | custom-call | tf_op jit(solution)/shard_map/pallas_call | solution.py:269
  93.7 1.0 %copy.5 = bf16[1,128,4096]{2,1,0:T(8,128)(2,1)} copy(bf16[1,128,4096]{2,1,0:T(8,128)(2,1)S(1)} %bitcast.12) | data formatting | bytes 2097152
Async XLA Ops:
  0.1 1.2 %copy-start = (bf16[1,128,4096]{2,1,0:T(8,128)(2,1)S(1)}, bf16[1,128,4096]{2,1,0:T(8,128)(2,1)}, u32[]{:S(2)}) copy-start(bf16[1,128,4096]{2,1,0:T(8,128)(2,1)} %param.3) | copy-start | bytes 3145732
  1.3 0.9 %copy-start.1 = (bf16[2,1,128,512]{3,2,1,0:T(8,128)(2,1)S(1)}, bf16[2,1,128,512]{3,2,1,0:T(8,128)(2,1)}, u32[]{:S(2)}) copy-start(bf16[2,1,128,512]{3,2,1,0:T(8,128)(2,1)} %param.4) | copy-start | bytes 786436
  2.3 0.7 copy-start.2
